TPU v7x, 1024 devices: a whole 4x8x16 slice. The times are simulated.
1024 devices in a mesh: term: 128 (over y, z), blk: 8 (over x, core).
Axes of the slice: x: 4, y: 8, z: 16, core: 2. Of those that a mesh axis runs over, the one named last changes fastest.
Arguments:
- psi: bfloat16 [2, 8, 512, 448], P(None, 'blk'), may hold values from -6 to 6
- left_env: bfloat16 [128, 8, 512, 512], P('term', 'blk'), may hold values from -0.03125 to 0.03125
- right_env: bfloat16 [128, 8, 448, 448], P('term', 'blk'), may hold values from -0.375 to 0.375
- source: int32 [128, 8], P('term', 'blk'), may hold values from 0 to 7
- left_size: int32 [8], replicated, may hold values from 64 to 512
- right_size: int32 [8], replicated, may hold values from 64 to 448
Outputs:
- sigma: float32 [2, 8, 512, 448], P(None, 'blk', 'term')
All inputs are finite; a program needn't handle non-finite values.
Results may differ from a plain program's by a relative error of at most 0.0029.
Values may be sent and summed in bfloat16 or wider, within the bound.
No kernel may reach another device: no remote copies, remote signals or barrier semaphores. Data moves between devices by JAX's collectives and lax.ppermute only.
A program may use at most 32 MiB of HBM per device.

v0:
```python
import jax
import jax.numpy as jnp
from jax import lax
from jax.sharding import PartitionSpec as P


def local(psi, left_env, right_env, source, left_size, right_size):
    rows = psi.shape[2]
    cols = psi.shape[3]
    vectors = psi.shape[0]
    here = lax.axis_index("blk")
    target = source[0, 0]
    row_ids = jnp.arange(rows, dtype=jnp.int32)
    col_ids = jnp.arange(cols, dtype=jnp.int32)
    empty = jnp.zeros((vectors, rows, cols), psi.dtype)
    piece = lax.all_gather(psi, "blk", axis=1, tiled=True)
    count = piece.shape[1]
    inside = (target >= 0) & (target < count)
    chosen = lax.dynamic_index_in_dim(piece, jnp.clip(target, 0, count - 1), 1, keepdims=False)
    block = jnp.where(inside, chosen, empty)
    keep_in = (row_ids < left_size[target])[:, None] & (col_ids < right_size[target])[None, :]
    block = jnp.where(keep_in[None], block, jnp.zeros_like(block))
    keep_out = (row_ids < left_size[here])[:, None] & (col_ids < right_size[here])[None, :]
    left = left_env[0, 0]
    right = right_env[0, 0]
    middle = jnp.einsum("ab,vbc->avc", left, block, preferred_element_type=jnp.float32).astype(
        jnp.bfloat16
    )
    flat = middle.reshape(rows * vectors, cols)
    result = jnp.dot(flat, right, preferred_element_type=jnp.float32).reshape(rows, vectors, cols)
    shares = lax.psum_scatter(
        jnp.where(keep_out[:, None, :], result, jnp.zeros_like(result)),
        "term",
        scatter_dimension=0,
        tiled=True,
    )
    return jnp.transpose(shares, (1, 0, 2))[:, None]


def solution(mesh):
    return jax.shard_map(
        local,
        mesh=mesh,
        in_specs=(
            P(None, "blk", None, None),
            P("term", "blk", None, None),
            P("term", "blk", None, None),
            P("term", "blk"),
            P(),
            P(),
        ),
        out_specs=P(None, "blk", "term", None),
        check_vma=False,
    )
```

profile of v0, /device:TPU:2, one launch (start us, length us, event | category | flops | bytes accessed | tf_op | source)
XLA Modules:
  0.0 376.7 jit_solution(13138310417627818651)
XLA Ops:
  6.5 0.0 copy-start
  6.5 0.0 all-gather.2.cloned.1.call-start
  6.5 0.7 all-gather.2.cloned.1.call-update
  7.3 0.0 all-reduce.3.cloned.1.call-start
  8.0 1.4 fusion.22
  9.4 0.6 iota_compare_fusion.2
  10.0 0.6 iota_compare_fusion.3
  10.6 0.7 iota_compare_fusion
  11.3 0.7 iota_compare_fusion.1
  12.0 0.2 broadcast_and_fusion.1
  12.2 0.2 broadcast_and_fusion
  12.4 60.6 %all-gather.2.cloned.1.call-done = bf16[2,8,512,448]{2,3,1,0:T(8,128)(2,1)} async-done(((bf16[2,1,512,448]{2,3,1,0:T(8,128)(2,1)}), bf16[2,8,512,448]{2,3,1,0:T(8,128)(2,1)}) %all-gather.2.cloned.1.call-update) | async-done | bytes 7340048 | tf_op jit(solution)/shard_map/all_gather | solution.py:16
  73.0 0.0 copy-done
  73.0 4.0 %convolution_select_fusion = f32[512,2,448]{2,0,1:T(8,128)} fusion(pred[512,448]{1,0:T(8,128)(4,1)S(1)} %broadcast_and_fusion, bf16[2,8,512,448]{2,3,1,0:T(8,128)(2,1)} %all-gather.2.cloned.1.call-done, s32[]{:T(128)S(6)} %min.4, pred[]{:T(512)S(6)} %and.44, pred[512,448]{0,1:T(8,128)(4,1)S(1)} %broadcast_and_fusion.1, ...), kind=kOutput, calls=%fused_computation | convolution fusion | flops 882638848 | bytes 4194309 | tf_op jit(solution)/shard_map/dot_general | solution.py:30
  77.0 0.0 all-reduce.3.cloned.1.call-update
  77.0 1.3 dynamic-slice
  78.9 289.5 %all-reduce.3.cloned.1.call-done = f32[512,2,448]{2,0,1:T(8,128)} async-done(((f32[512,2,448]{2,0,1:T(8,128)}), f32[512,2,448]{2,0,1:T(8,128)}) %all-reduce.3.cloned.1.call-update) | async-done | bytes 1835024
  368.5 1.4 dynamic-slice_bitcast_fusion
Async XLA Ops:
  6.5 66.5 %copy-start = (bf16[1,1,512,512]{3,2,1,0:T(8,128)(2,1)S(1)}, bf16[1,1,512,512]{3,2,1,0:T(8,128)(2,1)}, u32[]{:S(2)}) copy-start(bf16[1,1,512,512]{3,2,1,0:T(8,128)(2,1)} %param.7) | copy-start | bytes 1572868
  6.5 66.4 %all-gather.2.cloned.1.call-start = ((), (), s32[]{:S(2)}) async-start(), calls=%async_computation | async-start | bytes 8257536 | tf_op jit(solution)/shard_map/all_gather | solution.py:16
  7.3 361.2 %all-reduce.3.cloned.1.call-start = ((), (), s32[]{:S(2)}) async-start(), calls=%async_computation.1 | async-start | bytes 4194304
Sparse Core Ops, SparseCore 0:
  10.1 62.8 all-gather.1
  77.1 291.3 all-reduce.2
where the time goes:
time: 377 us
  waiting for transfers between devices  351 us (93%)
  between operations  14.8 us (4%)
  local copies, waits for them, and re-layouts  4.05 us (1%)
  matrix products  3.99 us (1%)
    unnamed x3, waiting for transfers between devices  290 us
    all_gather x1, waiting for transfers between devices, local(): piece = lax.all_gather(psi, 'blk', axis=1, tiled=True)  60.6 us
  transfers between devices with their start and end apart: 2, of which 2 were waited for; matrix products, arithmetic and copies ran while one was open for 1% of the time, Pallas kernels for 0%

commit v1 on v0

v1 whole, which is shorter than its diff:
```python
import jax
import jax.numpy as jnp
from jax import lax
from jax.experimental import pallas as pl
from jax.experimental.pallas import tpu as pltpu
from jax.sharding import Mesh, PartitionSpec as P

VECTORS = 2


def pick_kernel(wanted, have, out):
    out[...] = have[...]


def pick(have, wanted):
    slots, rows, cols = have.shape
    return pl.pallas_call(
        pick_kernel,
        out_shape=jax.ShapeDtypeStruct((slots, rows, cols), have.dtype),
        grid_spec=pltpu.PrefetchScalarGridSpec(
            num_scalar_prefetch=1,
            grid=(slots,),
            in_specs=[pl.BlockSpec((1, rows, cols), lambda i, wanted: (wanted[i], 0, 0))],
            out_specs=pl.BlockSpec((1, rows, cols), lambda i, wanted: (i, 0, 0)),
        ),
        name="pick",
    )(wanted, have)


def apply_kernel(order, source, left_size, right_size, block, left, right, out):
    rows = left.shape[0]
    cols = right.shape[0]
    here = lax.axis_index("x") * lax.axis_size("core") + lax.axis_index("core")
    target = source[0, 0]
    out_row = lax.broadcasted_iota(jnp.int32, (rows, rows), 0)
    in_row = lax.broadcasted_iota(jnp.int32, (rows, rows), 1)
    keep = (order(out_row) == in_row) & (in_row < left_size[here])
    permute = jnp.where(keep, 1.0, 0.0).astype(left.dtype)
    live = lax.broadcasted_iota(jnp.int32, (rows, rows), 1) < left_size[target]
    lefts = jnp.where(live, left[...], jnp.zeros_like(left))
    lefts = jnp.dot(permute, lefts, preferred_element_type=jnp.float32).astype(left.dtype)
    row = lax.broadcasted_iota(jnp.int32, (cols, cols), 0)
    col = lax.broadcasted_iota(jnp.int32, (cols, cols), 1)
    live = (row < right_size[target]) & (col < right_size[here])
    rights = jnp.where(live, right[...], jnp.zeros_like(right))
    results = []
    for v in range(VECTORS):
        middle = lax.dot_general(
            lefts,
            block[v * cols : (v + 1) * cols, :],
            (((1,), (1,)), ((), ())),
            preferred_element_type=jnp.float32,
        ).astype(left.dtype)
        results.append(jnp.dot(middle, rights, preferred_element_type=jnp.float32))
    out[...] = jnp.concatenate(results, axis=1).astype(out.dtype)


def apply(order, source, left_size, right_size, block, left, right):
    rows = left.shape[0]
    cols = right.shape[0]
    smem = pl.BlockSpec(memory_space=pltpu.SMEM)
    vmem = pl.BlockSpec(memory_space=pltpu.VMEM)
    return pl.pallas_call(
        lambda *refs: apply_kernel(order, *refs),
        out_shape=jax.ShapeDtypeStruct((rows, VECTORS * cols), left.dtype),
        in_specs=[smem] * 3 + [vmem] * 3,
        out_specs=vmem,
        compiler_params=pltpu.CompilerParams(vmem_limit_bytes=32 * 1024 * 1024),
        name="apply",
    )(source, left_size, right_size, block, left, right)


def local(psi, left_env, right_env, source, left_size, right_size):
    size = lax.axis_size
    rows = psi.shape[2]
    cols = psi.shape[3]
    near = size("yl") * size("zl")
    far = size("yh") * size("zh")
    each = rows // (near * far)

    asked = lax.optimization_barrier(jnp.broadcast_to(source, (8, 128)))
    asked = lax.optimization_barrier(lax.all_gather(asked, ("core", "yl", "zl")))
    wanted = asked[:, 0, 0]

    share = cols // near
    part = lax.axis_index("yl") * size("zl") + lax.axis_index("zl")
    turned = jnp.transpose(psi[:, 0], (0, 2, 1))
    mine = lax.dynamic_slice_in_dim(turned, part * share, share, 1)
    sends = jnp.broadcast_to(mine[None], (size("x"),) + mine.shape)
    sends = sends.reshape(-1, share, rows)
    have = lax.all_to_all(sends, ("x", "core"), 0, 0)
    block = lax.all_to_all(pick(have, wanted), ("core", "yl", "zl"), 0, 0)
    block = block.reshape(VECTORS * cols, rows)

    def order(p):
        unit, last = p // each, p % each
        zh, unit = unit % size("zh"), unit // size("zh")
        yh, unit = unit % size("yh"), unit // size("yh")
        zl, yl = unit % size("zl"), unit // size("zl")
        term = ((yh * size("yl") + yl) * size("zh") + zh) * size("zl") + zl
        return term * each + last

    result = apply(order, source, left_size, right_size, block, left_env[0, 0], right_env[0, 0])
    result = result.reshape(near, rows // near, VECTORS * cols)
    got = lax.all_to_all(result, ("yl", "zl"), 0, 0)
    total = jnp.sum(got.astype(jnp.float32), axis=0).astype(jnp.bfloat16)
    got = lax.all_to_all(total.reshape(far, each, VECTORS * cols), ("yh", "zh"), 0, 0)
    total = jnp.sum(got.astype(jnp.float32), axis=0)
    return jnp.transpose(total.reshape(each, VECTORS, cols), (1, 0, 2))[:, None]


def solution(mesh):
    y, z = 8, 16
    shape = (y // 2, 2, z // 2, 2, 4, 2)
    fine = Mesh(mesh.devices.reshape(shape), ("yh", "yl", "zh", "zl", "x", "core"))
    term = ("yh", "yl", "zh", "zl")
    blk = ("x", "core")
    return jax.shard_map(
        local,
        mesh=fine,
        in_specs=(P(None, blk), P(term, blk), P(term, blk), P(term, blk), P(), P()),
        out_specs=P(None, blk, term),
        check_vma=False,
    )
```

time: 377 us -> 121 us (0.32)
  the two profiles are of different devices: /device:TPU:2 before, /device:TPU:10 now
where the time goes in v1:
time: 121 us; the launch traced here: 120 us
  blocking collectives  101 us (83%)
  Pallas kernels  8.24 us (7%)
  local copies, waits for them, and re-layouts  5.33 us (4%)
  starting transfers between devices  4.83 us (4%)
    all_to_all x1, blocking collectives, local(): lax.all_to_all(total.reshape(far, each, VECTORS * cols), ('yh', 'zh'), 0, 0)  34.6 us
    all_gather x1, blocking collectives, local(): lax.all_gather(asked, ('core', 'yl', 'zl'))  34 us
    all_to_all x1, blocking collectives, local(): block = lax.all_to_all(pick(have, wanted), ('core', 'yl', 'zl'), 0, 0)  16.6 us
    all_to_all x1, blocking collectives, local(): got = lax.all_to_all(result, ('yl', 'zl'), 0, 0)  15.9 us
    pallas_call x1, Pallas kernels, pick(): pl.pallas_call(pick_kernel, out_shape=jax.ShapeDtypeStruct((slots, rows,...  5.8 us
    all_to_all x1, starting transfers between devices, local(): have = lax.all_to_all(sends, ('x', 'core'), 0, 0)  4.83 us
    unnamed x12, local copies, waits for them, and re-layouts  2.78 us
    pallas_call x1, Pallas kernels, apply(): pl.pallas_call(lambda *refs: apply_kernel(order, *refs), out_shape=jax.Sh...  2.44 us
  transfers between devices with their start and end apart: 1, of which 0 were waited for; matrix products, arithmetic and copies ran while one was open for 1% of the time, Pallas kernels for 0%

profile of v1, /device:TPU:10, one launch (start us, length us, event | category | flops | bytes accessed | tf_op | source)
XLA Modules:
  0.0 120.5 jit_solution(4989120559248490438)
XLA Ops:
  0.0 0.0 copy-start
  0.0 1.2 copy-done
  1.2 1.0 broadcast_in_dim.18
  2.2 4.8 %all-to-all-start = ((bf16[8,112,512]{2,1,0:T(8,128)(2,1)}), bf16[8,112,512]{2,1,0:T(8,128)(2,1)S(1)}, u32[]{:S(2)}, u32[]{:S(2)}) async-start(bf16[8,112,512]{2,1,0:T(8,128)(2,1)} %bitcast.4), calls=%async_computation | async-start | bytes 1835008 | tf_op jit(solution)/shard_map/all_to_all | solution.py:91
  7.7 34.0 %all-gather = s32[64,128]{1,0:T(8,128)S(1)} all-gather(s32[8,128]{1,0:T(8,128)S(1)} %broadcast_in_dim.17), channel_id=2, replica_groups=mesh['yh'=4,'yl'=2,'zh'=8,'zl'=2,'x'=4,'core'=2] {'core','yl','zl'}, dimensions={0}, use_global_device_ids=true | all-gather | bytes 36864 | tf_op jit(solution)/shard_map/all_gather | solution.py:82
  41.7 0.8 slice_reduce_fusion.wanted
  42.5 0.0 all-to-all-done.have
  42.5 0.0 copy-start.5
  42.5 0.9 copy-done.5
  43.4 5.8 %pick.1 = bf16[8,112,512]{2,1,0:T(8,128)(2,1)} custom-call(s32[8]{0:T(128)} %slice_reduce_fusion.wanted, bf16[8,112,512]{2,1,0:T(8,128)(2,1)} %copy-done.5), custom_call_target="tpu_custom_call" | custom-call | tf_op jit(solution)/shard_map/pick/pallas_call | solution.py:17
  49.2 0.0 copy-start.1
  49.2 0.0 copy-start.2
  49.2 16.6 %all_to_all.20 = bf16[8,112,512]{2,1,0:T(8,128)(2,1)S(1)} all-to-all(bf16[8,112,512]{2,1,0:T(8,128)(2,1)} %pick.1), channel_id=1, replica_groups=mesh['yh'=4,'yl'=2,'zh'=8,'zl'=2,'x'=4,'core'=2] {'core','yl','zl'}, dimensions={0} | all-to-all | bytes 1835008 | tf_op jit(solution)/shard_map/all_to_all | solution.py:92
  65.9 0.0 copy-start.3
  65.9 0.0 copy-start.4
  65.9 0.0 copy-done.1
  65.9 0.0 copy-done.2
  65.9 0.6 copy-done.3
  66.5 0.0 copy-done.4
  66.6 2.4 %apply.1 = bf16[512,896]{1,0:T(8,128)(2,1)S(1)} custom-call(s32[1,1]{1,0:T(1,128)} %copy.17.refs_0_, s32[8]{0:T(128)S(1)} %copy-done.3, s32[8]{0:T(128)S(1)} %copy-done.4, bf16[896,512]{1,0:T(8,128)(2,1)S(1)} %bitcast.15, bf16[512,512]{1,0:T(8,128)(2,1)S(1)} %bitcast.17, bf16[448,448]{1,0:T(8,128)(2,1)S(1)} %bitcast.18), custom_call_target="tpu_custom_call" | custom-call | tf_op jit(solution)/shard_map/apply/pallas_call | solution.py:63
  69.0 15.9 %all_to_all.21 = bf16[4,128,896]{2,1,0:T(8,128)(2,1)S(1)} all-to-all(bf16[4,128,896]{2,1,0:T(8,128)(2,1)S(1)} %bitcast.16), channel_id=1, replica_groups=mesh['yh'=4,'yl'=2,'zh'=8,'zl'=2,'x'=4,'core'=2] {'yl','zl'}, dimensions={0} | all-to-all | bytes 1835008 | tf_op jit(solution)/shard_map/all_to_all | solution.py:105
  84.9 0.1 reduce_sum.21
  85.0 0.1 reshape.23
  85.1 34.6 %all_to_all.22 = bf16[32,4,896]{2,1,0:T(4,128)(2,1)S(1)} all-to-all(bf16[32,4,896]{2,1,0:T(4,128)(2,1)S(1)} %reshape.23), channel_id=1, replica_groups=mesh['yh'=4,'yl'=2,'zh'=8,'zl'=2,'x'=4,'core'=2] {'yh','zh'}, dimensions={0} | all-to-all | bytes 458752 | tf_op jit(solution)/shard_map/all_to_all | solution.py:107
  119.7 0.1 convert_reduce_fusion
  119.8 0.1 reshape.24
  119.9 0.6 copy.15
  (2 shorter events, 0.0 us)
Async XLA Ops:
  0.0 1.2 copy-start
  2.2 40.3 %all-to-all-start = ((bf16[8,112,512]{2,1,0:T(8,128)(2,1)}), bf16[8,112,512]{2,1,0:T(8,128)(2,1)S(1)}, u32[]{:S(2)}, u32[]{:S(2)}) async-start(bf16[8,112,512]{2,1,0:T(8,128)(2,1)} %bitcast.4), calls=%async_computation | async-start | bytes 1835008 | tf_op jit(solution)/shard_map/all_to_all | solution.py:91
  42.5 0.9 copy-start.5
  49.2 16.6 %copy-start.1 = (bf16[1,1,512,512]{3,2,1,0:T(8,128)(2,1)S(1)}, bf16[1,1,512,512]{3,2,1,0:T(8,128)(2,1)}, u32[]{:S(2)}) copy-start(bf16[1,1,512,512]{3,2,1,0:T(8,128)(2,1)} %param.7) | copy-start | bytes 1572868
  49.2 16.6 %copy-start.2 = (bf16[1,1,448,448]{3,2,1,0:T(8,128)(2,1)S(1)}, bf16[1,1,448,448]{3,2,1,0:T(8,128)(2,1)}, u32[]{:S(2)}) copy-start(bf16[1,1,448,448]{3,2,1,0:T(8,128)(2,1)} %param.8) | copy-start | bytes 1204228
  65.9 0.7 copy-start.3
  65.9 0.7 copy-start.4

commit v2 on v1

--- a/solution.py
+++ b/solution.py
@@ -9,20 +9,20 @@
 
 
 def pick_kernel(wanted, have, out):
-    out[...] = have[...]
+    for i in range(out.shape[0]):
+        out[i] = have[wanted[i]]
 
 
 def pick(have, wanted):
-    slots, rows, cols = have.shape
     return pl.pallas_call(
         pick_kernel,
-        out_shape=jax.ShapeDtypeStruct((slots, rows, cols), have.dtype),
-        grid_spec=pltpu.PrefetchScalarGridSpec(
-            num_scalar_prefetch=1,
-            grid=(slots,),
-            in_specs=[pl.BlockSpec((1, rows, cols), lambda i, wanted: (wanted[i], 0, 0))],
-            out_specs=pl.BlockSpec((1, rows, cols), lambda i, wanted: (i, 0, 0)),
-        ),
+        out_shape=jax.ShapeDtypeStruct(have.shape, have.dtype),
+        in_specs=[
+            pl.BlockSpec(memory_space=pltpu.SMEM),
+            pl.BlockSpec(memory_space=pltpu.VMEM),
+        ],
+        out_specs=pl.BlockSpec(memory_space=pltpu.VMEM),
+        compiler_params=pltpu.CompilerParams(vmem_limit_bytes=16 * 1024 * 1024),
         name="pick",
     )(wanted, have)
 
@@ -70,6 +70,20 @@
     )(source, left_size, right_size, block, left, right)
 
 
+def squares():
+    y, z, cores = (lax.axis_size(("yh", "yl")), lax.axis_size(("zh", "zl")), lax.axis_size("core"))
+    return [
+        [
+            (((a - 2 * core * yl) % y) * z + (b - 2 * core * zl) % z) * cores + core
+            for yl, a in enumerate((2 * yh, 2 * yh + 1))
+            for zl, b in enumerate((2 * zh, 2 * zh + 1))
+        ]
+        for yh in range(y // 2)
+        for zh in range(z // 2)
+        for core in range(cores)
+    ]
+
+
 def local(psi, left_env, right_env, source, left_size, right_size):
     size = lax.axis_size
     rows = psi.shape[2]
@@ -78,18 +92,19 @@
     far = size("yh") * size("zh")
     each = rows // (near * far)
 
-    asked = lax.optimization_barrier(jnp.broadcast_to(source, (8, 128)))
-    asked = lax.optimization_barrier(lax.all_gather(asked, ("core", "yl", "zl")))
-    wanted = asked[:, 0, 0]
-
     share = cols // near
     part = lax.axis_index("yl") * size("zl") + lax.axis_index("zl")
     turned = jnp.transpose(psi[:, 0], (0, 2, 1))
     mine = lax.dynamic_slice_in_dim(turned, part * share, share, 1)
     sends = jnp.broadcast_to(mine[None], (size("x"),) + mine.shape)
     sends = sends.reshape(-1, share, rows)
+    peers = ("core", "yl", "zl")
+    slots = size("core") * near
+    asked = jnp.where(jnp.arange(slots) == lax.axis_index(peers), source.reshape(1), 0)
+    sends, asked = lax.optimization_barrier((sends, asked))
     have = lax.all_to_all(sends, ("x", "core"), 0, 0)
-    block = lax.all_to_all(pick(have, wanted), ("core", "yl", "zl"), 0, 0)
+    wanted = lax.psum(asked, peers)
+    block = lax.all_to_all(pick(have, wanted), peers, 0, 0)
     block = block.reshape(VECTORS * cols, rows)
 
     def order(p):
@@ -102,7 +117,7 @@
 
     result = apply(order, source, left_size, right_size, block, left_env[0, 0], right_env[0, 0])
     result = result.reshape(near, rows // near, VECTORS * cols)
-    got = lax.all_to_all(result, ("yl", "zl"), 0, 0)
+    got = lax.all_to_all(result, ("yh", "yl", "zh", "zl", "core"), 0, 0, axis_index_groups=squares())
     total = jnp.sum(got.astype(jnp.float32), axis=0).astype(jnp.bfloat16)
     got = lax.all_to_all(total.reshape(far, each, VECTORS * cols), ("yh", "zh"), 0, 0)
     total = jnp.sum(got.astype(jnp.float32), axis=0)

time: 121 us -> 102 us (0.84)
  the two profiles are of different devices: /device:TPU:10 before, /device:TPU:1 now
where the time goes in v2:
time: 102 us; the launch traced here: 100 us
  blocking collectives  67.3 us (66%)
  starting transfers between devices  17.6 us (17%)
  waiting for transfers between devices  8.62 us (8%)
  Pallas kernels  3.04 us (3%)
  local copies, waits for them, and re-layouts  2.91 us (3%)
    all_to_all x1, blocking collectives, local(): lax.all_to_all(total.reshape(far, each, VECTORS * cols), ('yh', 'zh'), 0, 0)  27.5 us
    all_to_all x1, blocking collectives, local(): lax.all_to_all(result, ('yh', 'yl', 'zh', 'zl', 'core'), 0, 0, axis_index...  17.9 us
    all_to_all x1, starting transfers between devices, local(): have = lax.all_to_all(sends, ('x', 'core'), 0, 0)  17.6 us
    all_to_all x1, blocking collectives, local(): block = lax.all_to_all(pick(have, wanted), peers, 0, 0)  16.8 us
    all_to_all x1, waiting for transfers between devices, local(): have = lax.all_to_all(sends, ('x', 'core'), 0, 0)  8.62 us
    psum x1, blocking collectives, local(): wanted = lax.psum(asked, peers)  5.09 us
    pallas_call x1, Pallas kernels, apply(): pl.pallas_call(lambda *refs: apply_kernel(order, *refs), out_shape=jax.Sh...  2.44 us
  transfers between devices with their start and end apart: 1, of which 1 were waited for; matrix products, arithmetic and copies ran while one was open for 0% of the time, Pallas kernels for 0%

profile of v2, /device:TPU:1, one launch (start us, length us, event | category | flops | bytes accessed | tf_op | source)
XLA Modules:
  0.0 100.4 jit_solution(8155593500164311049)
XLA Ops:
  0.0 0.0 copy-start
  0.7 0.4 copy-done
  1.2 1.0 %broadcast_in_dim.23 = bf16[4,2,112,512]{3,2,1,0:T(8,128)(2,1)} broadcast(bf16[2,112,512]{2,1,0:T(8,128)(2,1)S(1)} %dynamic-slice_bitcast_fusion), dimensions={1,2,3} | broadcast | bytes 1146880 | tf_op jit(solution)/shard_map/broadcast_in_dim | solution.py:99
  2.2 17.6 %all-to-all-start = ((bf16[8,112,512]{2,1,0:T(8,128)(2,1)}), bf16[8,112,512]{2,1,0:T(8,128)(2,1)S(1)}, u32[]{:S(2)}, u32[]{:S(2)}) async-start(bf16[8,112,512]{2,1,0:T(8,128)(2,1)} %bitcast.2), calls=%async_computation | async-start | bytes 1835008 | tf_op jit(solution)/shard_map/all_to_all | solution.py:105
  19.8 5.1 %psum.7.wanted = s32[8]{0:T(128)S(1)} all-reduce(s32[8]{0:T(128)S(1)} %compare_select_fusion), channel_id=1, replica_groups=mesh['yh'=4,'yl'=2,'zh'=8,'zl'=2,'x'=4,'core'=2] {'core','yl','zl'}, use_global_device_ids=true, to_apply=%region_0.1 | all-reduce | flops 8 | bytes 64 | tf_op jit(solution)/shard_map/psum | solution.py:106
  24.9 8.6 %all-to-all-done.have = bf16[8,112,512]{2,1,0:T(8,128)(2,1)S(1)} async-done(((bf16[8,112,512]{2,1,0:T(8,128)(2,1)}), bf16[8,112,512]{2,1,0:T(8,128)(2,1)S(1)}, u32[]{:S(2)}, u32[]{:S(2)}) %all-to-all-start) | async-done | bytes 917536 | tf_op jit(solution)/shard_map/all_to_all | solution.py:105
  33.5 0.6 pick.1
  34.2 0.0 copy-start.1
  34.2 0.0 copy-start.2
  34.2 16.8 %all_to_all.20 = bf16[8,112,512]{2,1,0:T(8,128)(2,1)S(1)} all-to-all(bf16[8,112,512]{2,1,0:T(8,128)(2,1)S(1)} %pick.1), channel_id=1, replica_groups=mesh['yh'=4,'yl'=2,'zh'=8,'zl'=2,'x'=4,'core'=2] {'core','yl','zl'}, dimensions={0} | all-to-all | bytes 1835008 | tf_op jit(solution)/shard_map/all_to_all | solution.py:107
  51.0 0.0 copy-start.3
  51.0 0.0 copy-start.4
  51.0 0.0 copy-done.1
  51.0 0.0 copy-done.2
  51.0 0.6 copy-done.3
  51.6 0.0 copy-done.4
  51.6 2.4 %apply.1 = bf16[512,896]{1,0:T(8,128)(2,1)S(1)} custom-call(s32[1,1]{1,0:T(1,128)} %copy.16.refs_0_, s32[8]{0:T(128)S(1)} %copy-done.3, s32[8]{0:T(128)S(1)} %copy-done.4, bf16[896,512]{1,0:T(8,128)(2,1)S(1)} %bitcast.14, bf16[512,512]{1,0:T(8,128)(2,1)S(1)} %bitcast.16, bf16[448,448]{1,0:T(8,128)(2,1)S(1)} %bitcast.17), custom_call_target="tpu_custom_call" | custom-call | tf_op jit(solution)/shard_map/apply/pallas_call | solution.py:63
  54.1 17.9 %all_to_all.21 = bf16[4,128,896]{2,1,0:T(8,128)(2,1)S(1)} all-to-all(bf16[4,128,896]{2,1,0:T(8,128)(2,1)S(1)} %bitcast.15), channel_id=1, replica_groups={{0,8,128,136},{1,121,897,1017},{16,24,144,152},{17,9,913,905},{32,40,16..., dimensions={0} | all-to-all | bytes 1835008 | tf_op jit(solution)/shard_map/all_to_all | solution.py:120
  72.0 0.1 reduce_sum.21
  72.1 0.1 reshape.25
  72.2 27.5 %all_to_all.22 = bf16[32,4,896]{2,1,0:T(4,128)(2,1)S(1)} all-to-all(bf16[32,4,896]{2,1,0:T(4,128)(2,1)S(1)} %reshape.25), channel_id=1, replica_groups=mesh['yh'=4,'yl'=2,'zh'=8,'zl'=2,'x'=4,'core'=2] {'yh','zh'}, dimensions={0} | all-to-all | bytes 458752 | tf_op jit(solution)/shard_map/all_to_all | solution.py:122
  99.7 0.1 convert_reduce_fusion
  99.7 0.1 reshape.26
  99.8 0.6 copy.14
  (2 shorter events, 0.0 us)
Async XLA Ops:
  0.0 1.2 %copy-start = (bf16[2,1,512,448]{2,3,1,0:T(8,128)(2,1)S(1)}, bf16[2,1,512,448]{2,3,1,0:T(8,128)(2,1)}, u32[]{:S(2)}) copy-start(bf16[2,1,512,448]{2,3,1,0:T(8,128)(2,1)} %param.6) | copy-start | bytes 2752516
  2.2 31.3 %all-to-all-start = ((bf16[8,112,512]{2,1,0:T(8,128)(2,1)}), bf16[8,112,512]{2,1,0:T(8,128)(2,1)S(1)}, u32[]{:S(2)}, u32[]{:S(2)}) async-start(bf16[8,112,512]{2,1,0:T(8,128)(2,1)} %bitcast.2), calls=%async_computation | async-start | bytes 1835008 | tf_op jit(solution)/shard_map/all_to_all | solution.py:105
  34.2 16.8 %copy-start.1 = (bf16[1,1,512,512]{3,2,1,0:T(8,128)(2,1)S(1)}, bf16[1,1,512,512]{3,2,1,0:T(8,128)(2,1)}, u32[]{:S(2)}) copy-start(bf16[1,1,512,512]{3,2,1,0:T(8,128)(2,1)} %param.7) | copy-start | bytes 1572868
  34.2 16.8 %copy-start.2 = (bf16[1,1,448,448]{3,2,1,0:T(8,128)(2,1)S(1)}, bf16[1,1,448,448]{3,2,1,0:T(8,128)(2,1)}, u32[]{:S(2)}) copy-start(bf16[1,1,448,448]{3,2,1,0:T(8,128)(2,1)} %param.8) | copy-start | bytes 1204228
  51.0 0.7 copy-start.3
  51.0 0.7 copy-start.4

commit v3 on v2

--- a/solution.py
+++ b/solution.py
@@ -27,7 +27,7 @@
     )(wanted, have)
 
 
-def apply_kernel(order, source, left_size, right_size, block, left, right, out):
+def prepare_kernel(order, source, left_size, right_size, left, right, lefts, rights):
     rows = left.shape[0]
     cols = right.shape[0]
     here = lax.axis_index("x") * lax.axis_size("core") + lax.axis_index("core")
@@ -36,38 +36,73 @@
     in_row = lax.broadcasted_iota(jnp.int32, (rows, rows), 1)
     keep = (order(out_row) == in_row) & (in_row < left_size[here])
     permute = jnp.where(keep, 1.0, 0.0).astype(left.dtype)
-    live = lax.broadcasted_iota(jnp.int32, (rows, rows), 1) < left_size[target]
-    lefts = jnp.where(live, left[...], jnp.zeros_like(left))
-    lefts = jnp.dot(permute, lefts, preferred_element_type=jnp.float32).astype(left.dtype)
+    live = in_row < left_size[target]
+    masked = jnp.where(live, left[...], jnp.zeros_like(left))
+    lefts[...] = jnp.dot(permute, masked, preferred_element_type=jnp.float32).astype(left.dtype)
     row = lax.broadcasted_iota(jnp.int32, (cols, cols), 0)
     col = lax.broadcasted_iota(jnp.int32, (cols, cols), 1)
     live = (row < right_size[target]) & (col < right_size[here])
-    rights = jnp.where(live, right[...], jnp.zeros_like(right))
+    rights[...] = jnp.where(live, right[...], jnp.zeros_like(right))
+
+
+def prepare(order, source, left_size, right_size, left, right):
+    smem = pl.BlockSpec(memory_space=pltpu.SMEM)
+    vmem = pl.BlockSpec(memory_space=pltpu.VMEM)
+    rows = left.shape[0]
+    return pl.pallas_call(
+        lambda *refs: prepare_kernel(order, *refs),
+        out_shape=[jax.ShapeDtypeStruct(a.shape, a.dtype) for a in (left, right)],
+        in_specs=[smem] * 3 + [vmem] * 2,
+        out_specs=[vmem] * 2,
+        compiler_params=pltpu.CompilerParams(vmem_limit_bytes=16 * 1024 * 1024),
+        cost_estimate=pl.CostEstimate(flops=2 * rows**3, bytes_accessed=8 * rows * rows, transcendentals=0),
+        name="prepare",
+    )(source, left_size, right_size, left, right)
+
+
+def apply_kernel(block, lefts, rights, out):
+    cols = rights.shape[0]
     results = []
     for v in range(VECTORS):
         middle = lax.dot_general(
-            lefts,
+            lefts[...],
             block[v * cols : (v + 1) * cols, :],
             (((1,), (1,)), ((), ())),
             preferred_element_type=jnp.float32,
-        ).astype(left.dtype)
-        results.append(jnp.dot(middle, rights, preferred_element_type=jnp.float32))
+        ).astype(lefts.dtype)
+        results.append(jnp.dot(middle, rights[...], preferred_element_type=jnp.float32))
     out[...] = jnp.concatenate(results, axis=1).astype(out.dtype)
 
 
-def apply(order, source, left_size, right_size, block, left, right):
-    rows = left.shape[0]
-    cols = right.shape[0]
-    smem = pl.BlockSpec(memory_space=pltpu.SMEM)
+def apply(block, lefts, rights):
     vmem = pl.BlockSpec(memory_space=pltpu.VMEM)
     return pl.pallas_call(
-        lambda *refs: apply_kernel(order, *refs),
-        out_shape=jax.ShapeDtypeStruct((rows, VECTORS * cols), left.dtype),
-        in_specs=[smem] * 3 + [vmem] * 3,
+        apply_kernel,
+        out_shape=jax.ShapeDtypeStruct((lefts.shape[0], VECTORS * rights.shape[1]), lefts.dtype),
+        in_specs=[vmem] * 3,
         out_specs=vmem,
-        compiler_params=pltpu.CompilerParams(vmem_limit_bytes=32 * 1024 * 1024),
+        compiler_params=pltpu.CompilerParams(vmem_limit_bytes=24 * 1024 * 1024),
         name="apply",
-    )(source, left_size, right_size, block, left, right)
+    )(block, lefts, rights)
+
+
+def finish_kernel(parts, out):
+    total = jnp.sum(parts[...].astype(jnp.float32), axis=0)
+    cols = out.shape[-1]
+    for v in range(VECTORS):
+        out[v, 0] = total[:, v * cols : (v + 1) * cols]
+
+
+def finish(parts):
+    vmem = pl.BlockSpec(memory_space=pltpu.VMEM)
+    unused, each, cols = parts.shape
+    return pl.pallas_call(
+        finish_kernel,
+        out_shape=jax.ShapeDtypeStruct((VECTORS, 1, each, cols // VECTORS), jnp.float32),
+        in_specs=[vmem],
+        out_specs=vmem,
+        name="finish",
+    )(parts)
 
 
 def squares():
@@ -92,6 +127,14 @@
     far = size("yh") * size("zh")
     each = rows // (near * far)
 
+    def order(p):
+        unit, last = p // each, p % each
+        zh, unit = unit % size("zh"), unit // size("zh")
+        yh, unit = unit % size("yh"), unit // size("yh")
+        zl, yl = unit % size("zl"), unit // size("zl")
+        term = ((yh * size("yl") + yl) * size("zh") + zh) * size("zl") + zl
+        return term * each + last
+
     share = cols // near
     part = lax.axis_index("yl") * size("zl") + lax.axis_index("zl")
     turned = jnp.transpose(psi[:, 0], (0, 2, 1))
@@ -101,27 +144,20 @@
     peers = ("core", "yl", "zl")
     slots = size("core") * near
     asked = jnp.where(jnp.arange(slots) == lax.axis_index(peers), source.reshape(1), 0)
-    sends, asked = lax.optimization_barrier((sends, asked))
+    left, right = left_env[0, 0], right_env[0, 0]
+    sends, asked, left, right = lax.optimization_barrier((sends, asked, left, right))
     have = lax.all_to_all(sends, ("x", "core"), 0, 0)
     wanted = lax.psum(asked, peers)
+    lefts, rights = prepare(order, source, left_size, right_size, left, right)
     block = lax.all_to_all(pick(have, wanted), peers, 0, 0)
     block = block.reshape(VECTORS * cols, rows)
 
-    def order(p):
-        unit, last = p // each, p % each
-        zh, unit = unit % size("zh"), unit // size("zh")
-        yh, unit = unit % size("yh"), unit // size("yh")
-        zl, yl = unit % size("zl"), unit // size("zl")
-        term = ((yh * size("yl") + yl) * size("zh") + zh) * size("zl") + zl
-        return term * each + last
-
-    result = apply(order, source, left_size, right_size, block, left_env[0, 0], right_env[0, 0])
+    result = apply(block, lefts, rights)
     result = result.reshape(near, rows // near, VECTORS * cols)
     got = lax.all_to_all(result, ("yh", "yl", "zh", "zl", "core"), 0, 0, axis_index_groups=squares())
     total = jnp.sum(got.astype(jnp.float32), axis=0).astype(jnp.bfloat16)
     got = lax.all_to_all(total.reshape(far, each, VECTORS * cols), ("yh", "zh"), 0, 0)
-    total = jnp.sum(got.astype(jnp.float32), axis=0)
-    return jnp.transpose(total.reshape(each, VECTORS, cols), (1, 0, 2))[:, None]
+    return finish(got)
 
 
 def solution(mesh):

time: 102 us -> 102 us (level)
  the two profiles are of different devices: /device:TPU:1 before, /device:TPU:129 now
where the time goes in v3:
time: 102 us
  blocking collectives  65.9 us (65%)
  waiting for transfers between devices  16.1 us (16%)
  starting transfers between devices  10.6 us (10%)
  Pallas kernels  5.9 us (6%)
  local copies, waits for them, and re-layouts  2.56 us (3%)
    all_to_all x1, blocking collectives, local(): lax.all_to_all(total.reshape(far, each, VECTORS * cols), ('yh', 'zh'), 0, 0)  38.6 us
    all_to_all x1, blocking collectives, local(): lax.all_to_all(result, ('yh', 'yl', 'zh', 'zl', 'core'), 0, 0, axis_index...  18.8 us
    all_to_all x1, waiting for transfers between devices, local(): block = lax.all_to_all(pick(have, wanted), peers, 0, 0)  10.9 us
    psum x1, blocking collectives, local(): wanted = lax.psum(asked, peers)  8.48 us
    all_to_all x1, starting transfers between devices, local(): block = lax.all_to_all(pick(have, wanted), peers, 0, 0)  5.66 us
    all_to_all x1, waiting for transfers between devices, local(): have = lax.all_to_all(sends, ('x', 'core'), 0, 0)  5.21 us
    all_to_all x1, starting transfers between devices, local(): have = lax.all_to_all(sends, ('x', 'core'), 0, 0)  4.97 us
  transfers between devices with their start and end apart: 2, of which 2 were waited for; matrix products, arithmetic and copies ran while one was open for 0% of the time, Pallas kernels for 1%

profile of v3, /device:TPU:129, one launch (start us, length us, event | category | flops | bytes accessed | tf_op | source)
XLA Modules:
  0.0 102.0 jit_solution(14246801584481597329)
XLA Ops:
  0.0 0.0 copy-start
  0.7 0.4 copy-done
  1.2 1.0 broadcast_in_dim.20
  2.2 5.0 %all-to-all-start = ((bf16[8,112,512]{2,1,0:T(8,128)(2,1)}), bf16[8,112,512]{2,1,0:T(8,128)(2,1)S(1)}, u32[]{:S(2)}, u32[]{:S(2)}) async-start(bf16[8,112,512]{2,1,0:T(8,128)(2,1)} %bitcast.2), calls=%async_computation | async-start | bytes 1835008 | tf_op jit(solution)/shard_map/all_to_all | solution.py:149
  7.2 8.5 %psum.7.wanted = s32[8]{0:T(128)S(1)} all-reduce(s32[8]{0:T(128)S(1)} %compare_select_fusion), channel_id=1, replica_groups=mesh['yh'=4,'yl'=2,'zh'=8,'zl'=2,'x'=4,'core'=2] {'core','yl','zl'}, use_global_device_ids=true, to_apply=%region_0.1 | all-reduce | flops 8 | bytes 64 | tf_op jit(solution)/shard_map/psum | solution.py:150
  15.7 5.2 %all-to-all-done.have = bf16[8,112,512]{2,1,0:T(8,128)(2,1)S(1)} async-done(((bf16[8,112,512]{2,1,0:T(8,128)(2,1)}), bf16[8,112,512]{2,1,0:T(8,128)(2,1)S(1)}, u32[]{:S(2)}, u32[]{:S(2)}) %all-to-all-start) | async-done | bytes 917536 | tf_op jit(solution)/shard_map/all_to_all | solution.py:149
  20.9 1.5 %pick.1 = bf16[8,112,512]{2,1,0:T(8,128)(2,1)} custom-call(s32[8]{0:T(128)S(1)} %psum.7.wanted, bf16[8,112,512]{2,1,0:T(8,128)(2,1)S(1)} %all-to-all-done.have), custom_call_target="tpu_custom_call" | custom-call | tf_op jit(solution)/shard_map/pick/pallas_call | solution.py:17
  22.4 0.0 copy-start.1
  22.4 0.0 copy-start.3
  22.4 0.0 copy-start.4
  22.4 5.7 %all-to-all-start.1 = ((bf16[8,112,512]{2,1,0:T(8,128)(2,1)}), bf16[8,112,512]{2,1,0:T(8,128)(2,1)S(1)}, u32[]{:S(2)}, u32[]{:S(2)}) async-start(bf16[8,112,512]{2,1,0:T(8,128)(2,1)} %pick.1), calls=%async_computation.1 | async-start | bytes 1835008 | tf_op jit(solution)/shard_map/all_to_all | solution.py:152
  28.1 0.0 copy-done.1
  28.1 0.0 copy-done.3
  28.1 0.0 copy-done.4
  28.1 0.0 copy-start.2
  28.1 1.0 copy-done.2
  29.1 1.3 %prepare.1 = (bf16[512,512]{1,0:T(8,128)(2,1)S(1)}, bf16[448,448]{1,0:T(8,128)(2,1)S(1)}) custom-call(s32[1,1]{1,0:T(1,128)} %copy.7.refs_0_, s32[8]{0:T(128)S(1)} %copy-done.3, s32[8]{0:T(128)S(1)} %copy-done.4, bf16[512,512]{1,0:T(8,128)(2,1)S(1)} %bitcast.13, bf16[448,448]{1,0:T(8,128)(2,1)S(1)} %bitcast.14), custom_call_target="tpu_custom_call" | custom-call | flops 268435456 | bytes 2097152 | tf_op jit(solution)/shard_map/prepare/pallas_call | solution.py:52
  30.5 10.9 %all-to-all-done.1 = bf16[8,112,512]{2,1,0:T(8,128)(2,1)S(1)} async-done(((bf16[8,112,512]{2,1,0:T(8,128)(2,1)}), bf16[8,112,512]{2,1,0:T(8,128)(2,1)S(1)}, u32[]{:S(2)}, u32[]{:S(2)}) %all-to-all-start.1) | async-done | bytes 917536 | tf_op jit(solution)/shard_map/all_to_all | solution.py:152
  41.4 1.3 %apply.1 = bf16[512,896]{1,0:T(8,128)(2,1)S(1)} custom-call(bf16[896,512]{1,0:T(8,128)(2,1)S(1)} %bitcast.11, bf16[512,512]{1,0:T(8,128)(2,1)S(1)} %get-tuple-element.15.lefts, bf16[448,448]{1,0:T(8,128)(2,1)S(1)} %get-tuple-element.16.rights), custom_call_target="tpu_custom_call" | custom-call | tf_op jit(solution)/shard_map/apply/pallas_call | solution.py:79
  42.7 18.8 %all_to_all.20 = bf16[4,128,896]{2,1,0:T(8,128)(2,1)S(1)} all-to-all(bf16[4,128,896]{2,1,0:T(8,128)(2,1)S(1)} %bitcast.12), channel_id=1, replica_groups={{0,8,128,136},{1,121,897,1017},{16,24,144,152},{17,9,913,905},{32,40,16..., dimensions={0} | all-to-all | bytes 1835008 | tf_op jit(solution)/shard_map/all_to_all | solution.py:157
  61.5 0.1 reduce_sum.12
  61.7 0.1 reshape.22
  61.7 38.6 %all_to_all.21.parts = bf16[32,4,896]{2,1,0:T(4,128)(2,1)} all-to-all(bf16[32,4,896]{2,1,0:T(4,128)(2,1)S(1)} %reshape.22), channel_id=1, replica_groups=mesh['yh'=4,'yl'=2,'zh'=8,'zl'=2,'x'=4,'core'=2] {'yh','zh'}, dimensions={0} | all-to-all | bytes 458752 | tf_op jit(solution)/shard_map/all_to_all | solution.py:159
  100.3 1.7 %finish.1 = f32[2,1,4,448]{3,2,1,0:T(4,128)} custom-call(bf16[32,4,896]{2,1,0:T(4,128)(2,1)} %all_to_all.21.parts), custom_call_target="tpu_custom_call" | custom-call | tf_op jit(solution)/shard_map/finish/pallas_call | solution.py:99
  (2 shorter events, 0.0 us)
Async XLA Ops:
  0.0 1.2 %copy-start = (bf16[2,1,512,448]{2,3,1,0:T(8,128)(2,1)S(1)}, bf16[2,1,512,448]{2,3,1,0:T(8,128)(2,1)}, u32[]{:S(2)}) copy-start(bf16[2,1,512,448]{2,3,1,0:T(8,128)(2,1)} %param.6) | copy-start | bytes 2752516
  2.2 18.7 %all-to-all-start = ((bf16[8,112,512]{2,1,0:T(8,128)(2,1)}), bf16[8,112,512]{2,1,0:T(8,128)(2,1)S(1)}, u32[]{:S(2)}, u32[]{:S(2)}) async-start(bf16[8,112,512]{2,1,0:T(8,128)(2,1)} %bitcast.2), calls=%async_computation | async-start | bytes 1835008 | tf_op jit(solution)/shard_map/all_to_all | solution.py:149
  22.4 5.7 %copy-start.1 = (bf16[1,1,512,512]{3,2,1,0:T(8,128)(2,1)S(1)}, bf16[1,1,512,512]{3,2,1,0:T(8,128)(2,1)}, u32[]{:S(2)}) copy-start(bf16[1,1,512,512]{3,2,1,0:T(8,128)(2,1)} %param.7) | copy-start | bytes 1572868
  22.4 5.7 %copy-start.3 = (s32[8]{0:T(128)S(1)}, s32[8]{0:T(128)}, u32[]{:S(2)}) copy-start(s32[8]{0:T(128)} %refs_1_.1) | copy-start | bytes 100
  22.4 5.7 %copy-start.4 = (s32[8]{0:T(128)S(1)}, s32[8]{0:T(128)}, u32[]{:S(2)}) copy-start(s32[8]{0:T(128)} %refs_2_.1) | copy-start | bytes 100
  22.4 18.9 %all-to-all-start.1 = ((bf16[8,112,512]{2,1,0:T(8,128)(2,1)}), bf16[8,112,512]{2,1,0:T(8,128)(2,1)S(1)}, u32[]{:S(2)}, u32[]{:S(2)}) async-start(bf16[8,112,512]{2,1,0:T(8,128)(2,1)} %pick.1), calls=%async_computation.1 | async-start | bytes 1835008 | tf_op jit(solution)/shard_map/all_to_all | solution.py:152
  28.1 1.0 %copy-start.2 = (bf16[1,1,448,448]{3,2,1,0:T(8,128)(2,1)S(1)}, bf16[1,1,448,448]{3,2,1,0:T(8,128)(2,1)}, u32[]{:S(2)}) copy-start(bf16[1,1,448,448]{3,2,1,0:T(8,128)(2,1)} %param.8) | copy-start | bytes 1204228

commit v4 on v3

--- a/solution.py
+++ b/solution.py
@@ -86,25 +86,6 @@
     )(block, lefts, rights)
 
 
-def finish_kernel(parts, out):
-    total = jnp.sum(parts[...].astype(jnp.float32), axis=0)
-    cols = out.shape[-1]
-    for v in range(VECTORS):
-        out[v, 0] = total[:, v * cols : (v + 1) * cols]
-
-
-def finish(parts):
-    vmem = pl.BlockSpec(memory_space=pltpu.VMEM)
-    unused, each, cols = parts.shape
-    return pl.pallas_call(
-        finish_kernel,
-        out_shape=jax.ShapeDtypeStruct((VECTORS, 1, each, cols // VECTORS), jnp.float32),
-        in_specs=[vmem],
-        out_specs=vmem,
-        name="finish",
-    )(parts)
-
-
 def squares():
     y, z, cores = (lax.axis_size(("yh", "yl")), lax.axis_size(("zh", "zl")), lax.axis_size("core"))
     return [
@@ -149,7 +130,8 @@
     have = lax.all_to_all(sends, ("x", "core"), 0, 0)
     wanted = lax.psum(asked, peers)
     lefts, rights = prepare(order, source, left_size, right_size, left, right)
-    block = lax.all_to_all(pick(have, wanted), peers, 0, 0)
+    picked, lefts, rights = lax.optimization_barrier((pick(have, wanted), lefts, rights))
+    block = lax.all_to_all(picked, peers, 0, 0)
     block = block.reshape(VECTORS * cols, rows)
 
     result = apply(block, lefts, rights)
@@ -157,7 +139,8 @@
     got = lax.all_to_all(result, ("yh", "yl", "zh", "zl", "core"), 0, 0, axis_index_groups=squares())
     total = jnp.sum(got.astype(jnp.float32), axis=0).astype(jnp.bfloat16)
     got = lax.all_to_all(total.reshape(far, each, VECTORS * cols), ("yh", "zh"), 0, 0)
-    return finish(got)
+    total = jnp.sum(got.astype(jnp.float32), axis=0)
+    return jnp.transpose(total.reshape(each, VECTORS, cols), (1, 0, 2))[:, None]
 
 
 def solution(mesh):

time: 102 us -> 100 us (0.980)
  the two profiles are of different devices: /device:TPU:129 before, /device:TPU:1 now
where the time goes in v4:
time: 100 us; the launch traced here: 98.7 us
  blocking collectives  67.2 us (67%)
  starting transfers between devices  17.7 us (18%)
  waiting for transfers between devices  6.24 us (6%)
  Pallas kernels  3.28 us (3%)
  local copies, waits for them, and re-layouts  3.26 us (3%)
    all_to_all x1, blocking collectives, local(): lax.all_to_all(total.reshape(far, each, VECTORS * cols), ('yh', 'zh'), 0, 0)  27.5 us
    all_to_all x1, blocking collectives, local(): lax.all_to_all(result, ('yh', 'yl', 'zh', 'zl', 'core'), 0, 0, axis_index...  17.9 us
    all_to_all x1, starting transfers between devices, local(): have = lax.all_to_all(sends, ('x', 'core'), 0, 0)  17.7 us
    all_to_all x1, blocking collectives, local(): block = lax.all_to_all(picked, peers, 0, 0)  16.7 us
    all_to_all x1, waiting for transfers between devices, local(): have = lax.all_to_all(sends, ('x', 'core'), 0, 0)  6.24 us
    psum x1, blocking collectives, local(): wanted = lax.psum(asked, peers)  5.09 us
  transfers between devices with their start and end apart: 1, of which 1 were waited for; matrix products, arithmetic and copies ran while one was open for 0% of the time, Pallas kernels for 1%

profile of v4, /device:TPU:1, one launch (start us, length us, event | category | flops | bytes accessed | tf_op | source)
XLA Modules:
  0.0 98.7 jit_solution(4118412731543723215)
XLA Ops:
  0.0 0.0 copy-start
  0.7 0.4 copy-done
  1.2 1.0 %broadcast_in_dim.23 = bf16[4,2,112,512]{3,2,1,0:T(8,128)(2,1)} broadcast(bf16[2,112,512]{2,1,0:T(8,128)(2,1)S(1)} %dynamic-slice_bitcast_fusion), dimensions={1,2,3} | broadcast | bytes 1146880 | tf_op jit(solution)/shard_map/broadcast_in_dim | solution.py:123
  2.2 0.0 copy-start.1
  2.2 17.7 %all-to-all-start = ((bf16[8,112,512]{2,1,0:T(8,128)(2,1)}), bf16[8,112,512]{2,1,0:T(8,128)(2,1)S(1)}, u32[]{:S(2)}, u32[]{:S(2)}) async-start(bf16[8,112,512]{2,1,0:T(8,128)(2,1)} %bitcast.2), calls=%async_computation | async-start | bytes 1835008 | tf_op jit(solution)/shard_map/all_to_all | solution.py:130
  20.0 0.0 copy-start.3
  20.0 0.0 copy-start.4
  20.0 5.1 %psum.7.wanted = s32[8]{0:T(128)S(1)} all-reduce(s32[8]{0:T(128)S(1)} %compare_select_fusion), channel_id=1, replica_groups=mesh['yh'=4,'yl'=2,'zh'=8,'zl'=2,'x'=4,'core'=2] {'core','yl','zl'}, use_global_device_ids=true, to_apply=%region_0.1 | all-reduce | flops 8 | bytes 64 | tf_op jit(solution)/shard_map/psum | solution.py:131
  25.1 0.0 copy-done.1
  25.1 0.0 copy-done.3
  25.1 0.0 copy-done.4
  25.1 0.0 copy-start.2
  25.1 1.0 %copy-done.2 = bf16[1,1,448,448]{3,2,1,0:T(8,128)(2,1)S(1)} copy-done((bf16[1,1,448,448]{3,2,1,0:T(8,128)(2,1)S(1)}, bf16[1,1,448,448]{3,2,1,0:T(8,128)(2,1)}, u32[]{:S(2)}) %copy-start.2) | copy-done | bytes 401432
  26.1 1.3 %prepare.1 = (bf16[512,512]{1,0:T(8,128)(2,1)S(1)}, bf16[448,448]{1,0:T(8,128)(2,1)S(1)}) custom-call(s32[1,1]{1,0:T(1,128)} %copy.16.refs_0_, s32[8]{0:T(128)S(1)} %copy-done.3, s32[8]{0:T(128)S(1)} %copy-done.4, bf16[512,512]{1,0:T(8,128)(2,1)S(1)} %bitcast.16, bf16[448,448]{1,0:T(8,128)(2,1)S(1)} %bitcast.17), custom_call_target="tpu_custom_call" | custom-call | flops 268435456 | bytes 2097152 | tf_op jit(solution)/shard_map/prepare/pallas_call | solution.py:52
  27.4 6.2 %all-to-all-done.have = bf16[8,112,512]{2,1,0:T(8,128)(2,1)S(1)} async-done(((bf16[8,112,512]{2,1,0:T(8,128)(2,1)}), bf16[8,112,512]{2,1,0:T(8,128)(2,1)S(1)}, u32[]{:S(2)}, u32[]{:S(2)}) %all-to-all-start) | async-done | bytes 917536 | tf_op jit(solution)/shard_map/all_to_all | solution.py:130
  33.7 0.6 pick.1
  34.3 16.7 %all_to_all.20 = bf16[8,112,512]{2,1,0:T(8,128)(2,1)S(1)} all-to-all(bf16[8,112,512]{2,1,0:T(8,128)(2,1)S(1)} %pick.1), channel_id=1, replica_groups=mesh['yh'=4,'yl'=2,'zh'=8,'zl'=2,'x'=4,'core'=2] {'core','yl','zl'}, dimensions={0} | all-to-all | bytes 1835008 | tf_op jit(solution)/shard_map/all_to_all | solution.py:134
  50.9 1.3 %apply.1 = bf16[512,896]{1,0:T(8,128)(2,1)S(1)} custom-call(bf16[896,512]{1,0:T(8,128)(2,1)S(1)} %bitcast.14, bf16[512,512]{1,0:T(8,128)(2,1)S(1)} %get-tuple-element.21.lefts, bf16[448,448]{1,0:T(8,128)(2,1)S(1)} %get-tuple-element.22.rights), custom_call_target="tpu_custom_call" | custom-call | tf_op jit(solution)/shard_map/apply/pallas_call | solution.py:79
  52.3 17.9 %all_to_all.21 = bf16[4,128,896]{2,1,0:T(8,128)(2,1)S(1)} all-to-all(bf16[4,128,896]{2,1,0:T(8,128)(2,1)S(1)} %bitcast.15), channel_id=1, replica_groups={{0,8,128,136},{1,121,897,1017},{16,24,144,152},{17,9,913,905},{32,40,16..., dimensions={0} | all-to-all | bytes 1835008 | tf_op jit(solution)/shard_map/all_to_all | solution.py:139
  70.2 0.1 reduce_sum.21
  70.3 0.1 reshape.25
  70.4 27.5 %all_to_all.22 = bf16[32,4,896]{2,1,0:T(4,128)(2,1)S(1)} all-to-all(bf16[32,4,896]{2,1,0:T(4,128)(2,1)S(1)} %reshape.25), channel_id=1, replica_groups=mesh['yh'=4,'yl'=2,'zh'=8,'zl'=2,'x'=4,'core'=2] {'yh','zh'}, dimensions={0} | all-to-all | bytes 458752 | tf_op jit(solution)/shard_map/all_to_all | solution.py:141
  97.9 0.1 convert_reduce_fusion
  98.0 0.1 reshape.26
  98.1 0.6 copy.14
  (2 shorter events, 0.0 us)
Async XLA Ops:
  0.0 1.2 %copy-start = (bf16[2,1,512,448]{2,3,1,0:T(8,128)(2,1)S(1)}, bf16[2,1,512,448]{2,3,1,0:T(8,128)(2,1)}, u32[]{:S(2)}) copy-start(bf16[2,1,512,448]{2,3,1,0:T(8,128)(2,1)} %param.6) | copy-start | bytes 2752516
  2.2 22.8 %copy-start.1 = (bf16[1,1,512,512]{3,2,1,0:T(8,128)(2,1)S(1)}, bf16[1,1,512,512]{3,2,1,0:T(8,128)(2,1)}, u32[]{:S(2)}) copy-start(bf16[1,1,512,512]{3,2,1,0:T(8,128)(2,1)} %param.7) | copy-start | bytes 1572868
  2.2 31.5 %all-to-all-start = ((bf16[8,112,512]{2,1,0:T(8,128)(2,1)}), bf16[8,112,512]{2,1,0:T(8,128)(2,1)S(1)}, u32[]{:S(2)}, u32[]{:S(2)}) async-start(bf16[8,112,512]{2,1,0:T(8,128)(2,1)} %bitcast.2), calls=%async_computation | async-start | bytes 1835008 | tf_op jit(solution)/shard_map/all_to_all | solution.py:130
  20.0 5.1 %copy-start.3 = (s32[8]{0:T(128)S(1)}, s32[8]{0:T(128)}, u32[]{:S(2)}) copy-start(s32[8]{0:T(128)} %refs_1_.1) | copy-start | bytes 100
  20.0 5.1 %copy-start.4 = (s32[8]{0:T(128)S(1)}, s32[8]{0:T(128)}, u32[]{:S(2)}) copy-start(s32[8]{0:T(128)} %refs_2_.1) | copy-start | bytes 100
  25.1 1.0 %copy-start.2 = (bf16[1,1,448,448]{3,2,1,0:T(8,128)(2,1)S(1)}, bf16[1,1,448,448]{3,2,1,0:T(8,128)(2,1)}, u32[]{:S(2)}) copy-start(bf16[1,1,448,448]{3,2,1,0:T(8,128)(2,1)} %param.8) | copy-start | bytes 1204228

commit v5 on v4

--- a/solution.py
+++ b/solution.py
@@ -6,6 +6,7 @@
 from jax.sharding import Mesh, PartitionSpec as P
 
 VECTORS = 2
+STRIDE = 19
 
 
 def pick_kernel(wanted, have, out):
@@ -100,6 +101,24 @@
     ]
 
 
+def chip_at(place):
+    yh, zh = lax.axis_size("yh"), lax.axis_size("zh")
+    number = place * STRIDE % (yh * zh)
+    return number % yh, number // yh
+
+
+def strides():
+    z, cores = (lax.axis_size(("zh", "zl")), lax.axis_size("core"))
+    far = lax.axis_size("yh") * lax.axis_size("zh")
+    chips = [chip_at(place) for place in range(far)]
+    return [
+        [((2 * yh + yl) * z + 2 * zh + zl) * cores + core for yh, zh in chips]
+        for yl in range(lax.axis_size("yl"))
+        for zl in range(lax.axis_size("zl"))
+        for core in range(cores)
+    ]
+
+
 def local(psi, left_env, right_env, source, left_size, right_size):
     size = lax.axis_size
     rows = psi.shape[2]
@@ -110,9 +129,8 @@
 
     def order(p):
         unit, last = p // each, p % each
-        zh, unit = unit % size("zh"), unit // size("zh")
-        yh, unit = unit % size("yh"), unit // size("yh")
-        zl, yl = unit % size("zl"), unit // size("zl")
+        yh, zh = chip_at(unit % far)
+        zl, yl = unit // far % size("zl"), unit // far // size("zl")
         term = ((yh * size("yl") + yl) * size("zh") + zh) * size("zl") + zl
         return term * each + last
 
@@ -138,7 +156,8 @@
     result = result.reshape(near, rows // near, VECTORS * cols)
     got = lax.all_to_all(result, ("yh", "yl", "zh", "zl", "core"), 0, 0, axis_index_groups=squares())
     total = jnp.sum(got.astype(jnp.float32), axis=0).astype(jnp.bfloat16)
-    got = lax.all_to_all(total.reshape(far, each, VECTORS * cols), ("yh", "zh"), 0, 0)
+    parts = total.reshape(far, each, VECTORS * cols)
+    got = lax.all_to_all(parts, ("yh", "yl", "zh", "zl", "core"), 0, 0, axis_index_groups=strides())
     total = jnp.sum(got.astype(jnp.float32), axis=0)
     return jnp.transpose(total.reshape(each, VECTORS, cols), (1, 0, 2))[:, None]
 

time: 100 us -> 101 us (1.010)
  blocking collectives: 67.2 us -> 69.1 us
    all_to_all x1, blocking collectives: 27.5 us -> 29.4 us  [local(): lax.all_to_all(parts, ('yh', 'yl', 'zh', 'zl', 'core'), 0, 0, axis_index_...]
where the time goes in v5:
time: 101 us
  blocking collectives  69.1 us (68%)
  starting transfers between devices  17.7 us (18%)
  waiting for transfers between devices  6.15 us (6%)
  Pallas kernels  3.37 us (3%)
  local copies, waits for them, and re-layouts  3.26 us (3%)
    all_to_all x1, blocking collectives, local(): lax.all_to_all(parts, ('yh', 'yl', 'zh', 'zl', 'core'), 0, 0, axis_index_...  29.4 us
    all_to_all x1, blocking collectives, local(): lax.all_to_all(result, ('yh', 'yl', 'zh', 'zl', 'core'), 0, 0, axis_index...  17.9 us
    all_to_all x1, starting transfers between devices, local(): have = lax.all_to_all(sends, ('x', 'core'), 0, 0)  17.7 us
    all_to_all x1, blocking collectives, local(): block = lax.all_to_all(picked, peers, 0, 0)  16.7 us
    all_to_all x1, waiting for transfers between devices, local(): have = lax.all_to_all(sends, ('x', 'core'), 0, 0)  6.15 us
    psum x1, blocking collectives, local(): wanted = lax.psum(asked, peers)  5.09 us
  transfers between devices with their start and end apart: 1, of which 1 were waited for; matrix products, arithmetic and copies ran while one was open for 0% of the time, Pallas kernels for 1%

profile of v5, /device:TPU:1, one launch (start us, length us, event | category | flops | bytes accessed | tf_op | source)
XLA Modules:
  0.0 100.6 jit_solution(4979967203344931590)
XLA Ops:
  0.0 0.0 copy-start
  0.7 0.4 copy-done
  1.2 1.0 %broadcast_in_dim.23 = bf16[4,2,112,512]{3,2,1,0:T(8,128)(2,1)} broadcast(bf16[2,112,512]{2,1,0:T(8,128)(2,1)S(1)} %dynamic-slice_bitcast_fusion), dimensions={1,2,3} | broadcast | bytes 1146880 | tf_op jit(solution)/shard_map/broadcast_in_dim | solution.py:141
  2.2 0.0 copy-start.1
  2.2 17.7 %all-to-all-start = ((bf16[8,112,512]{2,1,0:T(8,128)(2,1)}), bf16[8,112,512]{2,1,0:T(8,128)(2,1)S(1)}, u32[]{:S(2)}, u32[]{:S(2)}) async-start(bf16[8,112,512]{2,1,0:T(8,128)(2,1)} %bitcast.2), calls=%async_computation | async-start | bytes 1835008 | tf_op jit(solution)/shard_map/all_to_all | solution.py:148
  20.0 0.0 copy-start.3
  20.0 0.0 copy-start.4
  20.0 5.1 %psum.7.wanted = s32[8]{0:T(128)S(1)} all-reduce(s32[8]{0:T(128)S(1)} %compare_select_fusion), channel_id=1, replica_groups=mesh['yh'=4,'yl'=2,'zh'=8,'zl'=2,'x'=4,'core'=2] {'core','yl','zl'}, use_global_device_ids=true, to_apply=%region_0.1 | all-reduce | flops 8 | bytes 64 | tf_op jit(solution)/shard_map/psum | solution.py:149
  25.1 0.0 copy-done.1
  25.1 0.0 copy-done.3
  25.1 0.0 copy-done.4
  25.1 0.0 copy-start.2
  25.1 1.0 %copy-done.2 = bf16[1,1,448,448]{3,2,1,0:T(8,128)(2,1)S(1)} copy-done((bf16[1,1,448,448]{3,2,1,0:T(8,128)(2,1)S(1)}, bf16[1,1,448,448]{3,2,1,0:T(8,128)(2,1)}, u32[]{:S(2)}) %copy-start.2) | copy-done | bytes 401432
  26.1 1.4 %prepare.1 = (bf16[512,512]{1,0:T(8,128)(2,1)S(1)}, bf16[448,448]{1,0:T(8,128)(2,1)S(1)}) custom-call(s32[1,1]{1,0:T(1,128)} %copy.16.refs_0_, s32[8]{0:T(128)S(1)} %copy-done.3, s32[8]{0:T(128)S(1)} %copy-done.4, bf16[512,512]{1,0:T(8,128)(2,1)S(1)} %bitcast.16, bf16[448,448]{1,0:T(8,128)(2,1)S(1)} %bitcast.17), custom_call_target="tpu_custom_call" | custom-call | flops 268435456 | bytes 2097152 | tf_op jit(solution)/shard_map/prepare/pallas_call | solution.py:53
  27.5 6.2 %all-to-all-done.have = bf16[8,112,512]{2,1,0:T(8,128)(2,1)S(1)} async-done(((bf16[8,112,512]{2,1,0:T(8,128)(2,1)}), bf16[8,112,512]{2,1,0:T(8,128)(2,1)S(1)}, u32[]{:S(2)}, u32[]{:S(2)}) %all-to-all-start) | async-done | bytes 917536 | tf_op jit(solution)/shard_map/all_to_all | solution.py:148
  33.7 0.6 pick.1
  34.3 16.7 %all_to_all.20 = bf16[8,112,512]{2,1,0:T(8,128)(2,1)S(1)} all-to-all(bf16[8,112,512]{2,1,0:T(8,128)(2,1)S(1)} %pick.1), channel_id=1, replica_groups=mesh['yh'=4,'yl'=2,'zh'=8,'zl'=2,'x'=4,'core'=2] {'core','yl','zl'}, dimensions={0} | all-to-all | bytes 1835008 | tf_op jit(solution)/shard_map/all_to_all | solution.py:152
  50.9 1.3 %apply.1 = bf16[512,896]{1,0:T(8,128)(2,1)S(1)} custom-call(bf16[896,512]{1,0:T(8,128)(2,1)S(1)} %bitcast.14, bf16[512,512]{1,0:T(8,128)(2,1)S(1)} %get-tuple-element.21.lefts, bf16[448,448]{1,0:T(8,128)(2,1)S(1)} %get-tuple-element.22.rights), custom_call_target="tpu_custom_call" | custom-call | tf_op jit(solution)/shard_map/apply/pallas_call | solution.py:80
  52.3 17.9 %all_to_all.21 = bf16[4,128,896]{2,1,0:T(8,128)(2,1)S(1)} all-to-all(bf16[4,128,896]{2,1,0:T(8,128)(2,1)S(1)} %bitcast.15), channel_id=1, replica_groups={{0,8,128,136},{1,121,897,1017},{16,24,144,152},{17,9,913,905},{32,40,16..., dimensions={0} | all-to-all | bytes 1835008 | tf_op jit(solution)/shard_map/all_to_all | solution.py:157
  70.2 0.1 reduce_sum.21
  70.3 0.1 reshape.25
  70.4 29.4 %all_to_all.22 = bf16[32,4,896]{2,1,0:T(4,128)(2,1)S(1)} all-to-all(bf16[32,4,896]{2,1,0:T(4,128)(2,1)S(1)} %reshape.25), channel_id=1, replica_groups={{0,832,528,352,48,880,576,272,96,800,624,320,16,848,544,368,64,768,592,..., dimensions={0} | all-to-all | bytes 458752 | tf_op jit(solution)/shard_map/all_to_all | solution.py:160
  99.8 0.1 convert_reduce_fusion
  99.9 0.1 reshape.26
  100.0 0.6 copy.14
  (2 shorter events, 0.0 us)
Async XLA Ops:
  0.0 1.2 %copy-start = (bf16[2,1,512,448]{2,3,1,0:T(8,128)(2,1)S(1)}, bf16[2,1,512,448]{2,3,1,0:T(8,128)(2,1)}, u32[]{:S(2)}) copy-start(bf16[2,1,512,448]{2,3,1,0:T(8,128)(2,1)} %param.6) | copy-start | bytes 2752516
  2.2 22.8 %copy-start.1 = (bf16[1,1,512,512]{3,2,1,0:T(8,128)(2,1)S(1)}, bf16[1,1,512,512]{3,2,1,0:T(8,128)(2,1)}, u32[]{:S(2)}) copy-start(bf16[1,1,512,512]{3,2,1,0:T(8,128)(2,1)} %param.7) | copy-start | bytes 1572868
  2.2 31.5 %all-to-all-start = ((bf16[8,112,512]{2,1,0:T(8,128)(2,1)}), bf16[8,112,512]{2,1,0:T(8,128)(2,1)S(1)}, u32[]{:S(2)}, u32[]{:S(2)}) async-start(bf16[8,112,512]{2,1,0:T(8,128)(2,1)} %bitcast.2), calls=%async_computation | async-start | bytes 1835008 | tf_op jit(solution)/shard_map/all_to_all | solution.py:148
  20.0 5.1 %copy-start.3 = (s32[8]{0:T(128)S(1)}, s32[8]{0:T(128)}, u32[]{:S(2)}) copy-start(s32[8]{0:T(128)} %refs_1_.1) | copy-start | bytes 100
  20.0 5.1 %copy-start.4 = (s32[8]{0:T(128)S(1)}, s32[8]{0:T(128)}, u32[]{:S(2)}) copy-start(s32[8]{0:T(128)} %refs_2_.1) | copy-start | bytes 100
  25.1 1.0 %copy-start.2 = (bf16[1,1,448,448]{3,2,1,0:T(8,128)(2,1)S(1)}, bf16[1,1,448,448]{3,2,1,0:T(8,128)(2,1)}, u32[]{:S(2)}) copy-start(bf16[1,1,448,448]{3,2,1,0:T(8,128)(2,1)} %param.8) | copy-start | bytes 1204228

commit v6 on v5

--- a/solution.py
+++ b/solution.py
@@ -6,7 +6,7 @@
 from jax.sharding import Mesh, PartitionSpec as P
 
 VECTORS = 2
-STRIDE = 19
+STRIDE = 29
 
 
 def pick_kernel(wanted, have, out):

time: 101 us -> 99.7 us (0.987); the launches traced: 101 us -> 98.1 us
  blocking collectives: 69.1 us -> 66.6 us
    all_to_all x1, blocking collectives: 29.4 us -> 26.9 us  [local(): lax.all_to_all(parts, ('yh', 'yl', 'zh', 'zl', 'core'), 0, 0, axis_index_...]
where the time goes in v6:
time: 99.7 us; the launch traced here: 98.1 us
  blocking collectives  66.6 us (67%)
  starting transfers between devices  17.7 us (18%)
  waiting for transfers between devices  6.15 us (6%)
  Pallas kernels  3.37 us (3%)
  local copies, waits for them, and re-layouts  3.26 us (3%)
    all_to_all x1, blocking collectives, local(): lax.all_to_all(parts, ('yh', 'yl', 'zh', 'zl', 'core'), 0, 0, axis_index_...  26.9 us
    all_to_all x1, blocking collectives, local(): lax.all_to_all(result, ('yh', 'yl', 'zh', 'zl', 'core'), 0, 0, axis_index...  17.9 us
    all_to_all x1, starting transfers between devices, local(): have = lax.all_to_all(sends, ('x', 'core'), 0, 0)  17.7 us
    all_to_all x1, blocking collectives, local(): block = lax.all_to_all(picked, peers, 0, 0)  16.7 us
    all_to_all x1, waiting for transfers between devices, local(): have = lax.all_to_all(sends, ('x', 'core'), 0, 0)  6.15 us
    psum x1, blocking collectives, local(): wanted = lax.psum(asked, peers)  5.09 us
  transfers between devices with their start and end apart: 1, of which 1 were waited for; matrix products, arithmetic and copies ran while one was open for 0% of the time, Pallas kernels for 1%

profile of v6, /device:TPU:1, one launch (start us, length us, event | category | flops | bytes accessed | tf_op | source)
XLA Modules:
  0.0 98.1 jit_solution(16512224690347848358)
XLA Ops:
  0.0 0.0 copy-start
  0.7 0.4 copy-done
  1.2 1.0 %broadcast_in_dim.23 = bf16[4,2,112,512]{3,2,1,0:T(8,128)(2,1)} broadcast(bf16[2,112,512]{2,1,0:T(8,128)(2,1)S(1)} %dynamic-slice_bitcast_fusion), dimensions={1,2,3} | broadcast | bytes 1146880 | tf_op jit(solution)/shard_map/broadcast_in_dim | solution.py:141
  2.2 0.0 copy-start.1
  2.2 17.7 %all-to-all-start = ((bf16[8,112,512]{2,1,0:T(8,128)(2,1)}), bf16[8,112,512]{2,1,0:T(8,128)(2,1)S(1)}, u32[]{:S(2)}, u32[]{:S(2)}) async-start(bf16[8,112,512]{2,1,0:T(8,128)(2,1)} %bitcast.2), calls=%async_computation | async-start | bytes 1835008 | tf_op jit(solution)/shard_map/all_to_all | solution.py:148
  20.0 0.0 copy-start.3
  20.0 0.0 copy-start.4
  20.0 5.1 %psum.7.wanted = s32[8]{0:T(128)S(1)} all-reduce(s32[8]{0:T(128)S(1)} %compare_select_fusion), channel_id=1, replica_groups=mesh['yh'=4,'yl'=2,'zh'=8,'zl'=2,'x'=4,'core'=2] {'core','yl','zl'}, use_global_device_ids=true, to_apply=%region_0.1 | all-reduce | flops 8 | bytes 64 | tf_op jit(solution)/shard_map/psum | solution.py:149
  25.1 0.0 copy-done.1
  25.1 0.0 copy-done.3
  25.1 0.0 copy-done.4
  25.1 0.0 copy-start.2
  25.1 1.0 %copy-done.2 = bf16[1,1,448,448]{3,2,1,0:T(8,128)(2,1)S(1)} copy-done((bf16[1,1,448,448]{3,2,1,0:T(8,128)(2,1)S(1)}, bf16[1,1,448,448]{3,2,1,0:T(8,128)(2,1)}, u32[]{:S(2)}) %copy-start.2) | copy-done | bytes 401432
  26.1 1.4 %prepare.1 = (bf16[512,512]{1,0:T(8,128)(2,1)S(1)}, bf16[448,448]{1,0:T(8,128)(2,1)S(1)}) custom-call(s32[1,1]{1,0:T(1,128)} %copy.16.refs_0_, s32[8]{0:T(128)S(1)} %copy-done.3, s32[8]{0:T(128)S(1)} %copy-done.4, bf16[512,512]{1,0:T(8,128)(2,1)S(1)} %bitcast.16, bf16[448,448]{1,0:T(8,128)(2,1)S(1)} %bitcast.17), custom_call_target="tpu_custom_call" | custom-call | flops 268435456 | bytes 2097152 | tf_op jit(solution)/shard_map/prepare/pallas_call | solution.py:53
  27.5 6.2 %all-to-all-done.have = bf16[8,112,512]{2,1,0:T(8,128)(2,1)S(1)} async-done(((bf16[8,112,512]{2,1,0:T(8,128)(2,1)}), bf16[8,112,512]{2,1,0:T(8,128)(2,1)S(1)}, u32[]{:S(2)}, u32[]{:S(2)}) %all-to-all-start) | async-done | bytes 917536 | tf_op jit(solution)/shard_map/all_to_all | solution.py:148
  33.7 0.6 pick.1
  34.3 16.7 %all_to_all.20 = bf16[8,112,512]{2,1,0:T(8,128)(2,1)S(1)} all-to-all(bf16[8,112,512]{2,1,0:T(8,128)(2,1)S(1)} %pick.1), channel_id=1, replica_groups=mesh['yh'=4,'yl'=2,'zh'=8,'zl'=2,'x'=4,'core'=2] {'core','yl','zl'}, dimensions={0} | all-to-all | bytes 1835008 | tf_op jit(solution)/shard_map/all_to_all | solution.py:152
  50.9 1.3 %apply.1 = bf16[512,896]{1,0:T(8,128)(2,1)S(1)} custom-call(bf16[896,512]{1,0:T(8,128)(2,1)S(1)} %bitcast.14, bf16[512,512]{1,0:T(8,128)(2,1)S(1)} %get-tuple-element.21.lefts, bf16[448,448]{1,0:T(8,128)(2,1)S(1)} %get-tuple-element.22.rights), custom_call_target="tpu_custom_call" | custom-call | tf_op jit(solution)/shard_map/apply/pallas_call | solution.py:80
  52.3 17.9 %all_to_all.21 = bf16[4,128,896]{2,1,0:T(8,128)(2,1)S(1)} all-to-all(bf16[4,128,896]{2,1,0:T(8,128)(2,1)S(1)} %bitcast.15), channel_id=1, replica_groups={{0,8,128,136},{1,121,897,1017},{16,24,144,152},{17,9,913,905},{32,40,16..., dimensions={0} | all-to-all | bytes 1835008 | tf_op jit(solution)/shard_map/all_to_all | solution.py:157
  70.2 0.1 reduce_sum.21
  70.3 0.1 reshape.25
  70.4 26.9 %all_to_all.22 = bf16[32,4,896]{2,1,0:T(4,128)(2,1)S(1)} all-to-all(bf16[32,4,896]{2,1,0:T(4,128)(2,1)S(1)} %reshape.25), channel_id=1, replica_groups={{0,368,608,848,80,320,560,800,32,272,512,880,112,352,592,832,64,304,544..., dimensions={0} | all-to-all | bytes 458752 | tf_op jit(solution)/shard_map/all_to_all | solution.py:160
  97.3 0.1 convert_reduce_fusion
  97.4 0.1 reshape.26
  97.5 0.6 copy.14
  (2 shorter events, 0.0 us)
Async XLA Ops:
  0.0 1.2 %copy-start = (bf16[2,1,512,448]{2,3,1,0:T(8,128)(2,1)S(1)}, bf16[2,1,512,448]{2,3,1,0:T(8,128)(2,1)}, u32[]{:S(2)}) copy-start(bf16[2,1,512,448]{2,3,1,0:T(8,128)(2,1)} %param.6) | copy-start | bytes 2752516
  2.2 22.8 %copy-start.1 = (bf16[1,1,512,512]{3,2,1,0:T(8,128)(2,1)S(1)}, bf16[1,1,512,512]{3,2,1,0:T(8,128)(2,1)}, u32[]{:S(2)}) copy-start(bf16[1,1,512,512]{3,2,1,0:T(8,128)(2,1)} %param.7) | copy-start | bytes 1572868
  2.2 31.5 %all-to-all-start = ((bf16[8,112,512]{2,1,0:T(8,128)(2,1)}), bf16[8,112,512]{2,1,0:T(8,128)(2,1)S(1)}, u32[]{:S(2)}, u32[]{:S(2)}) async-start(bf16[8,112,512]{2,1,0:T(8,128)(2,1)} %bitcast.2), calls=%async_computation | async-start | bytes 1835008 | tf_op jit(solution)/shard_map/all_to_all | solution.py:148
  20.0 5.1 %copy-start.3 = (s32[8]{0:T(128)S(1)}, s32[8]{0:T(128)}, u32[]{:S(2)}) copy-start(s32[8]{0:T(128)} %refs_1_.1) | copy-start | bytes 100
  20.0 5.1 %copy-start.4 = (s32[8]{0:T(128)S(1)}, s32[8]{0:T(128)}, u32[]{:S(2)}) copy-start(s32[8]{0:T(128)} %refs_2_.1) | copy-start | bytes 100
  25.1 1.0 %copy-start.2 = (bf16[1,1,448,448]{3,2,1,0:T(8,128)(2,1)S(1)}, bf16[1,1,448,448]{3,2,1,0:T(8,128)(2,1)}, u32[]{:S(2)}) copy-start(bf16[1,1,448,448]{3,2,1,0:T(8,128)(2,1)} %param.8) | copy-start | bytes 1204228

commit v7 on v6

--- a/solution.py
+++ b/solution.py
@@ -138,14 +138,15 @@
     part = lax.axis_index("yl") * size("zl") + lax.axis_index("zl")
     turned = jnp.transpose(psi[:, 0], (0, 2, 1))
     mine = lax.dynamic_slice_in_dim(turned, part * share, share, 1)
-    sends = jnp.broadcast_to(mine[None], (size("x"),) + mine.shape)
+    sends = jnp.broadcast_to(mine[:, None], (size("core"), size("x"), share, rows))
     sends = sends.reshape(-1, share, rows)
     peers = ("core", "yl", "zl")
     slots = size("core") * near
-    asked = jnp.where(jnp.arange(slots) == lax.axis_index(peers), source.reshape(1), 0)
+    place = source.reshape(1) % size("core") * size("x") + source.reshape(1) // size("core")
+    asked = jnp.where(jnp.arange(slots) == lax.axis_index(peers), place, 0)
     left, right = left_env[0, 0], right_env[0, 0]
     sends, asked, left, right = lax.optimization_barrier((sends, asked, left, right))
-    have = lax.all_to_all(sends, ("x", "core"), 0, 0)
+    have = lax.all_to_all(sends, ("core", "x"), 0, 0)
     wanted = lax.psum(asked, peers)
     lefts, rights = prepare(order, source, left_size, right_size, left, right)
     picked, lefts, rights = lax.optimization_barrier((pick(have, wanted), lefts, rights))

time: 99.7 us -> 99 us (level)
  no operation moved by 1% of the time
where the time goes in v7:
time: 99 us; the launch traced here: 97.5 us
  blocking collectives  66 us (67%)
  starting transfers between devices  17.8 us (18%)
  waiting for transfers between devices  6.04 us (6%)
  Pallas kernels  3.37 us (3%)
  local copies, waits for them, and re-layouts  3.23 us (3%)
    all_to_all x1, blocking collectives, local(): lax.all_to_all(parts, ('yh', 'yl', 'zh', 'zl', 'core'), 0, 0, axis_index_...  26.9 us
    all_to_all x1, blocking collectives, local(): lax.all_to_all(result, ('yh', 'yl', 'zh', 'zl', 'core'), 0, 0, axis_index...  17.9 us
    all_to_all x1, starting transfers between devices, local(): have = lax.all_to_all(sends, ('core', 'x'), 0, 0)  17.8 us
    all_to_all x1, blocking collectives, local(): block = lax.all_to_all(picked, peers, 0, 0)  16.1 us
    all_to_all x1, waiting for transfers between devices, local(): have = lax.all_to_all(sends, ('core', 'x'), 0, 0)  6.04 us
    psum x1, blocking collectives, local(): wanted = lax.psum(asked, peers)  5.06 us
  transfers between devices with their start and end apart: 1, of which 1 were waited for; matrix products, arithmetic and copies ran while one was open for 0% of the time, Pallas kernels for 1%

profile of v7, /device:TPU:1, one launch (start us, length us, event | category | flops | bytes accessed | tf_op | source)
XLA Modules:
  0.0 97.5 jit_solution(8903986225091137214)
XLA Ops:
  0.0 0.0 copy-start
  0.8 0.4 copy-done
  1.2 1.0 %broadcast_in_dim.23 = bf16[2,4,112,512]{3,2,1,0:T(8,128)(2,1)} broadcast(bf16[2,112,512]{2,1,0:T(8,128)(2,1)S(1)} %dynamic-slice_bitcast_fusion), dimensions={0,2,3} | broadcast | bytes 1146880 | tf_op jit(solution)/shard_map/broadcast_in_dim | solution.py:141
  2.2 0.0 copy-start.1
  2.2 17.8 %all-to-all-start = ((bf16[8,112,512]{2,1,0:T(8,128)(2,1)}), bf16[8,112,512]{2,1,0:T(8,128)(2,1)S(1)}, u32[]{:S(2)}, u32[]{:S(2)}) async-start(bf16[8,112,512]{2,1,0:T(8,128)(2,1)} %bitcast.2), calls=%async_computation | async-start | bytes 1835008 | tf_op jit(solution)/shard_map/all_to_all | solution.py:149
  20.0 0.0 copy-start.3
  20.0 0.0 copy-start.4
  20.0 5.1 %psum.7.wanted = s32[8]{0:T(128)S(1)} all-reduce(s32[8]{0:T(128)S(1)} %compare_select_fusion), channel_id=1, replica_groups=mesh['yh'=4,'yl'=2,'zh'=8,'zl'=2,'x'=4,'core'=2] {'core','yl','zl'}, use_global_device_ids=true, to_apply=%region_0.1 | all-reduce | flops 8 | bytes 64 | tf_op jit(solution)/shard_map/psum | solution.py:150
  25.1 0.0 copy-done.1
  25.1 0.0 copy-done.3
  25.1 0.0 copy-done.4
  25.1 0.0 copy-start.2
  25.1 1.0 %copy-done.2 = bf16[1,1,448,448]{3,2,1,0:T(8,128)(2,1)S(1)} copy-done((bf16[1,1,448,448]{3,2,1,0:T(8,128)(2,1)S(1)}, bf16[1,1,448,448]{3,2,1,0:T(8,128)(2,1)}, u32[]{:S(2)}) %copy-start.2) | copy-done | bytes 401432
  26.1 1.4 %prepare.1 = (bf16[512,512]{1,0:T(8,128)(2,1)S(1)}, bf16[448,448]{1,0:T(8,128)(2,1)S(1)}) custom-call(s32[1,1]{1,0:T(1,128)} %copy.16.refs_0_, s32[8]{0:T(128)S(1)} %copy-done.3, s32[8]{0:T(128)S(1)} %copy-done.4, bf16[512,512]{1,0:T(8,128)(2,1)S(1)} %bitcast.20, bf16[448,448]{1,0:T(8,128)(2,1)S(1)} %bitcast.21), custom_call_target="tpu_custom_call" | custom-call | flops 268435456 | bytes 2097152 | tf_op jit(solution)/shard_map/prepare/pallas_call | solution.py:53
  27.5 6.0 %all-to-all-done.have = bf16[8,112,512]{2,1,0:T(8,128)(2,1)S(1)} async-done(((bf16[8,112,512]{2,1,0:T(8,128)(2,1)}), bf16[8,112,512]{2,1,0:T(8,128)(2,1)S(1)}, u32[]{:S(2)}, u32[]{:S(2)}) %all-to-all-start) | async-done | bytes 917536 | tf_op jit(solution)/shard_map/all_to_all | solution.py:149
  33.6 0.6 pick.1
  34.2 16.1 %all_to_all.20 = bf16[8,112,512]{2,1,0:T(8,128)(2,1)S(1)} all-to-all(bf16[8,112,512]{2,1,0:T(8,128)(2,1)S(1)} %pick.1), channel_id=1, replica_groups=mesh['yh'=4,'yl'=2,'zh'=8,'zl'=2,'x'=4,'core'=2] {'core','yl','zl'}, dimensions={0} | all-to-all | bytes 1835008 | tf_op jit(solution)/shard_map/all_to_all | solution.py:153
  50.3 1.3 %apply.1 = bf16[512,896]{1,0:T(8,128)(2,1)S(1)} custom-call(bf16[896,512]{1,0:T(8,128)(2,1)S(1)} %bitcast.18, bf16[512,512]{1,0:T(8,128)(2,1)S(1)} %get-tuple-element.21.lefts, bf16[448,448]{1,0:T(8,128)(2,1)S(1)} %get-tuple-element.22.rights), custom_call_target="tpu_custom_call" | custom-call | tf_op jit(solution)/shard_map/apply/pallas_call | solution.py:80
  51.7 17.9 %all_to_all.21 = bf16[4,128,896]{2,1,0:T(8,128)(2,1)S(1)} all-to-all(bf16[4,128,896]{2,1,0:T(8,128)(2,1)S(1)} %bitcast.19), channel_id=1, replica_groups={{0,8,128,136},{1,121,897,1017},{16,24,144,152},{17,9,913,905},{32,40,16..., dimensions={0} | all-to-all | bytes 1835008 | tf_op jit(solution)/shard_map/all_to_all | solution.py:158
  69.6 0.1 reduce_sum.21
  69.7 0.1 reshape.32
  69.8 26.9 %all_to_all.22 = bf16[32,4,896]{2,1,0:T(4,128)(2,1)S(1)} all-to-all(bf16[32,4,896]{2,1,0:T(4,128)(2,1)S(1)} %reshape.32), channel_id=1, replica_groups={{0,368,608,848,80,320,560,800,32,272,512,880,112,352,592,832,64,304,544..., dimensions={0} | all-to-all | bytes 458752 | tf_op jit(solution)/shard_map/all_to_all | solution.py:161
  96.7 0.1 convert_reduce_fusion
  96.8 0.1 reshape.33
  96.9 0.6 copy.14
  (2 shorter events, 0.0 us)
Async XLA Ops:
  0.0 1.2 %copy-start = (bf16[2,1,512,448]{2,3,1,0:T(8,128)(2,1)S(1)}, bf16[2,1,512,448]{2,3,1,0:T(8,128)(2,1)}, u32[]{:S(2)}) copy-start(bf16[2,1,512,448]{2,3,1,0:T(8,128)(2,1)} %param.6) | copy-start | bytes 2752516
  2.2 22.8 %copy-start.1 = (bf16[1,1,512,512]{3,2,1,0:T(8,128)(2,1)S(1)}, bf16[1,1,512,512]{3,2,1,0:T(8,128)(2,1)}, u32[]{:S(2)}) copy-start(bf16[1,1,512,512]{3,2,1,0:T(8,128)(2,1)} %param.7) | copy-start | bytes 1572868
  2.2 31.3 %all-to-all-start = ((bf16[8,112,512]{2,1,0:T(8,128)(2,1)}), bf16[8,112,512]{2,1,0:T(8,128)(2,1)S(1)}, u32[]{:S(2)}, u32[]{:S(2)}) async-start(bf16[8,112,512]{2,1,0:T(8,128)(2,1)} %bitcast.2), calls=%async_computation | async-start | bytes 1835008 | tf_op jit(solution)/shard_map/all_to_all | solution.py:149
  20.0 5.1 %copy-start.3 = (s32[8]{0:T(128)S(1)}, s32[8]{0:T(128)}, u32[]{:S(2)}) copy-start(s32[8]{0:T(128)} %refs_1_.1) | copy-start | bytes 100
  20.0 5.1 %copy-start.4 = (s32[8]{0:T(128)S(1)}, s32[8]{0:T(128)}, u32[]{:S(2)}) copy-start(s32[8]{0:T(128)} %refs_2_.1) | copy-start | bytes 100
  25.1 1.0 %copy-start.2 = (bf16[1,1,448,448]{3,2,1,0:T(8,128)(2,1)S(1)}, bf16[1,1,448,448]{3,2,1,0:T(8,128)(2,1)}, u32[]{:S(2)}) copy-start(bf16[1,1,448,448]{3,2,1,0:T(8,128)(2,1)} %param.8) | copy-start | bytes 1204228

commit v8 on v7

--- a/solution.py
+++ b/solution.py
@@ -6,7 +6,7 @@
 from jax.sharding import Mesh, PartitionSpec as P
 
 VECTORS = 2
-STRIDE = 29
+STRIDE = 25
 
 
 def pick_kernel(wanted, have, out):

time: 99 us -> 99.1 us (level); the launches traced: 97.5 us -> 98.7 us
  blocking collectives: 66 us -> 67.3 us
    all_to_all x1, blocking collectives: 26.9 us -> 28.2 us  [local(): lax.all_to_all(parts, ('yh', 'yl', 'zh', 'zl', 'core'), 0, 0, axis_index_...]
where the time goes in v8:
time: 99.1 us; the launch traced here: 98.7 us
  blocking collectives  67.3 us (68%)
  starting transfers between devices  17.8 us (18%)
  waiting for transfers between devices  6.04 us (6%)
  Pallas kernels  3.37 us (3%)
  local copies, waits for them, and re-layouts  3.23 us (3%)
    all_to_all x1, blocking collectives, local(): lax.all_to_all(parts, ('yh', 'yl', 'zh', 'zl', 'core'), 0, 0, axis_index_...  28.2 us
    all_to_all x1, blocking collectives, local(): lax.all_to_all(result, ('yh', 'yl', 'zh', 'zl', 'core'), 0, 0, axis_index...  17.9 us
    all_to_all x1, starting transfers between devices, local(): have = lax.all_to_all(sends, ('core', 'x'), 0, 0)  17.8 us
    all_to_all x1, blocking collectives, local(): block = lax.all_to_all(picked, peers, 0, 0)  16.1 us
    all_to_all x1, waiting for transfers between devices, local(): have = lax.all_to_all(sends, ('core', 'x'), 0, 0)  6.04 us
    psum x1, blocking collectives, local(): wanted = lax.psum(asked, peers)  5.06 us
  transfers between devices with their start and end apart: 1, of which 1 were waited for; matrix products, arithmetic and copies ran while one was open for 0% of the time, Pallas kernels for 1%

profile of v8, /device:TPU:1, one launch (start us, length us, event | category | flops | bytes accessed | tf_op | source)
XLA Modules:
  0.0 98.7 jit_solution(8851183336800987846)
XLA Ops:
  0.0 0.0 copy-start
  0.8 0.4 copy-done
  1.2 1.0 %broadcast_in_dim.23 = bf16[2,4,112,512]{3,2,1,0:T(8,128)(2,1)} broadcast(bf16[2,112,512]{2,1,0:T(8,128)(2,1)S(1)} %dynamic-slice_bitcast_fusion), dimensions={0,2,3} | broadcast | bytes 1146880 | tf_op jit(solution)/shard_map/broadcast_in_dim | solution.py:141
  2.2 0.0 copy-start.1
  2.2 17.8 %all-to-all-start = ((bf16[8,112,512]{2,1,0:T(8,128)(2,1)}), bf16[8,112,512]{2,1,0:T(8,128)(2,1)S(1)}, u32[]{:S(2)}, u32[]{:S(2)}) async-start(bf16[8,112,512]{2,1,0:T(8,128)(2,1)} %bitcast.2), calls=%async_computation | async-start | bytes 1835008 | tf_op jit(solution)/shard_map/all_to_all | solution.py:149
  20.0 0.0 copy-start.3
  20.0 0.0 copy-start.4
  20.0 5.1 %psum.7.wanted = s32[8]{0:T(128)S(1)} all-reduce(s32[8]{0:T(128)S(1)} %compare_select_fusion), channel_id=1, replica_groups=mesh['yh'=4,'yl'=2,'zh'=8,'zl'=2,'x'=4,'core'=2] {'core','yl','zl'}, use_global_device_ids=true, to_apply=%region_0.1 | all-reduce | flops 8 | bytes 64 | tf_op jit(solution)/shard_map/psum | solution.py:150
  25.1 0.0 copy-done.1
  25.1 0.0 copy-done.3
  25.1 0.0 copy-done.4
  25.1 0.0 copy-start.2
  25.1 1.0 %copy-done.2 = bf16[1,1,448,448]{3,2,1,0:T(8,128)(2,1)S(1)} copy-done((bf16[1,1,448,448]{3,2,1,0:T(8,128)(2,1)S(1)}, bf16[1,1,448,448]{3,2,1,0:T(8,128)(2,1)}, u32[]{:S(2)}) %copy-start.2) | copy-done | bytes 401432
  26.1 1.4 %prepare.1 = (bf16[512,512]{1,0:T(8,128)(2,1)S(1)}, bf16[448,448]{1,0:T(8,128)(2,1)S(1)}) custom-call(s32[1,1]{1,0:T(1,128)} %copy.16.refs_0_, s32[8]{0:T(128)S(1)} %copy-done.3, s32[8]{0:T(128)S(1)} %copy-done.4, bf16[512,512]{1,0:T(8,128)(2,1)S(1)} %bitcast.20, bf16[448,448]{1,0:T(8,128)(2,1)S(1)} %bitcast.21), custom_call_target="tpu_custom_call" | custom-call | flops 268435456 | bytes 2097152 | tf_op jit(solution)/shard_map/prepare/pallas_call | solution.py:53
  27.5 6.0 %all-to-all-done.have = bf16[8,112,512]{2,1,0:T(8,128)(2,1)S(1)} async-done(((bf16[8,112,512]{2,1,0:T(8,128)(2,1)}), bf16[8,112,512]{2,1,0:T(8,128)(2,1)S(1)}, u32[]{:S(2)}, u32[]{:S(2)}) %all-to-all-start) | async-done | bytes 917536 | tf_op jit(solution)/shard_map/all_to_all | solution.py:149
  33.6 0.6 pick.1
  34.2 16.1 %all_to_all.20 = bf16[8,112,512]{2,1,0:T(8,128)(2,1)S(1)} all-to-all(bf16[8,112,512]{2,1,0:T(8,128)(2,1)S(1)} %pick.1), channel_id=1, replica_groups=mesh['yh'=4,'yl'=2,'zh'=8,'zl'=2,'x'=4,'core'=2] {'core','yl','zl'}, dimensions={0} | all-to-all | bytes 1835008 | tf_op jit(solution)/shard_map/all_to_all | solution.py:153
  50.3 1.3 %apply.1 = bf16[512,896]{1,0:T(8,128)(2,1)S(1)} custom-call(bf16[896,512]{1,0:T(8,128)(2,1)S(1)} %bitcast.18, bf16[512,512]{1,0:T(8,128)(2,1)S(1)} %get-tuple-element.21.lefts, bf16[448,448]{1,0:T(8,128)(2,1)S(1)} %get-tuple-element.22.rights), custom_call_target="tpu_custom_call" | custom-call | tf_op jit(solution)/shard_map/apply/pallas_call | solution.py:80
  51.7 17.9 %all_to_all.21 = bf16[4,128,896]{2,1,0:T(8,128)(2,1)S(1)} all-to-all(bf16[4,128,896]{2,1,0:T(8,128)(2,1)S(1)} %bitcast.19), channel_id=1, replica_groups={{0,8,128,136},{1,121,897,1017},{16,24,144,152},{17,9,913,905},{32,40,16..., dimensions={0} | all-to-all | bytes 1835008 | tf_op jit(solution)/shard_map/all_to_all | solution.py:158
  69.6 0.1 reduce_sum.21
  69.7 0.1 reshape.32
  69.8 28.2 %all_to_all.22 = bf16[32,4,896]{2,1,0:T(4,128)(2,1)S(1)} all-to-all(bf16[32,4,896]{2,1,0:T(4,128)(2,1)S(1)} %reshape.32), channel_id=1, replica_groups={{0,352,576,800,16,368,592,816,32,256,608,832,48,272,624,848,64,288,512,..., dimensions={0} | all-to-all | bytes 458752 | tf_op jit(solution)/shard_map/all_to_all | solution.py:161
  98.0 0.1 convert_reduce_fusion
  98.0 0.1 reshape.33
  98.1 0.6 copy.14
  (2 shorter events, 0.0 us)
Async XLA Ops:
  0.0 1.2 %copy-start = (bf16[2,1,512,448]{2,3,1,0:T(8,128)(2,1)S(1)}, bf16[2,1,512,448]{2,3,1,0:T(8,128)(2,1)}, u32[]{:S(2)}) copy-start(bf16[2,1,512,448]{2,3,1,0:T(8,128)(2,1)} %param.6) | copy-start | bytes 2752516
  2.2 22.8 %copy-start.1 = (bf16[1,1,512,512]{3,2,1,0:T(8,128)(2,1)S(1)}, bf16[1,1,512,512]{3,2,1,0:T(8,128)(2,1)}, u32[]{:S(2)}) copy-start(bf16[1,1,512,512]{3,2,1,0:T(8,128)(2,1)} %param.7) | copy-start | bytes 1572868
  2.2 31.3 %all-to-all-start = ((bf16[8,112,512]{2,1,0:T(8,128)(2,1)}), bf16[8,112,512]{2,1,0:T(8,128)(2,1)S(1)}, u32[]{:S(2)}, u32[]{:S(2)}) async-start(bf16[8,112,512]{2,1,0:T(8,128)(2,1)} %bitcast.2), calls=%async_computation | async-start | bytes 1835008 | tf_op jit(solution)/shard_map/all_to_all | solution.py:149
  20.0 5.1 %copy-start.3 = (s32[8]{0:T(128)S(1)}, s32[8]{0:T(128)}, u32[]{:S(2)}) copy-start(s32[8]{0:T(128)} %refs_1_.1) | copy-start | bytes 100
  20.0 5.1 %copy-start.4 = (s32[8]{0:T(128)S(1)}, s32[8]{0:T(128)}, u32[]{:S(2)}) copy-start(s32[8]{0:T(128)} %refs_2_.1) | copy-start | bytes 100
  25.1 1.0 %copy-start.2 = (bf16[1,1,448,448]{3,2,1,0:T(8,128)(2,1)S(1)}, bf16[1,1,448,448]{3,2,1,0:T(8,128)(2,1)}, u32[]{:S(2)}) copy-start(bf16[1,1,448,448]{3,2,1,0:T(8,128)(2,1)} %param.8) | copy-start | bytes 1204228
